TPU v7x, 128 devices: a whole 4x4x4 slice. The times are simulated.
128 devices in a mesh: dp: 8 (over x, core), mp: 16 (over z, y).
Axes of the slice: x: 4, y: 4, z: 4, core: 2. Of those that a mesh axis runs over, the one named last changes fastest.
Arguments:
- gradient: float32 [256, 512, 512], P('mp', 'dp')
- owner: int32 [256], replicated, may hold values from 0 to 127, as said below
- stat_left: float32 [8, 16, 3, 512, 512], P('dp', 'mp'), as said below
- stat_right: float32 [8, 16, 3, 512, 512], P('dp', 'mp'), as said below
- root_left: bfloat16 [8, 16, 3, 512, 512], P('dp', 'mp'), as said below
- root_right: bfloat16 [8, 16, 3, 512, 512], P('dp', 'mp'), as said below
Outputs:
- preconditioned: float32 [256, 512, 512], P('mp', 'dp')
- new_stat_left: float32 [8, 16, 3, 512, 512], P('dp', 'mp')
- new_stat_right: float32 [8, 16, 3, 512, 512], P('dp', 'mp')
- new_root_left: bfloat16 [8, 16, 3, 512, 512], P('dp', 'mp')
- new_root_right: bfloat16 [8, 16, 3, 512, 512], P('dp', 'mp')
Inputs may be any that keep to these rules, and one draw needn't show every extreme that they name: Each entry is a device e * 16 + h. Of the blocks of set g, exactly one has its owner's mp index equal to h, for every g and h. Every device owns at most 3 blocks and some device of every mp index owns exactly 3. `stat_left`: each matrix is symmetric with a positive diagonal that exceeds the sum of the magnitudes of its row's other entries. `stat_right`: each matrix is symmetric with a positive diagonal that exceeds the sum of the magnitudes of its row's other entries. `root_left`: each matrix is symmetric. `root_right`: each matrix is symmetric.
All inputs are finite; a program needn't handle non-finite values.
Results may differ from a plain program's by a relative error of at most 0.001.
Values sent between devices are 32-bit elements; how exact they have to be, the bound alone decides.
A program may use at most 192 MiB of HBM per device.

v0:
```python
import jax
import jax.numpy as jnp
from jax import lax
from jax.sharding import PartitionSpec as P

decay_rate = 0.95
damping = 0.001


def matmul_high(left_matrix, right_matrix):
    return jnp.matmul(left_matrix, right_matrix, precision=lax.Precision.HIGHEST)


def newton_step(statistic, old_root):
    size_order = statistic.shape[0]
    identity = jnp.eye(size_order, dtype=jnp.float32)
    scale = jnp.trace(statistic) / size_order
    shifted = statistic / scale + damping * identity
    square = matmul_high(old_root, old_root)
    power = matmul_high(matmul_high(square, square), shifted)
    return matmul_high(old_root, (5.0 * identity - power) / 4.0)


def refresh_block(grad_block, old_left, old_right, prev_left, prev_right):
    left_new = decay_rate * old_left + matmul_high(grad_block, grad_block.T)
    right_new = decay_rate * old_right + matmul_high(grad_block.T, grad_block)
    inverse_left = newton_step(left_new, prev_left.astype(jnp.float32))
    inverse_right = newton_step(right_new, prev_right.astype(jnp.float32))
    result = matmul_high(matmul_high(inverse_left, grad_block), inverse_right)
    return (
        result,
        left_new,
        right_new,
        inverse_left.astype(jnp.bfloat16),
        inverse_right.astype(jnp.bfloat16),
    )


def select_rows(source, index, live):
    picked = jnp.take(source, index, axis=0)
    return jnp.where(live[:, None, None], picked, jnp.zeros_like(picked))


def inverse_table(targets, count):
    matches = targets[None, :] == jnp.arange(count, dtype=jnp.int32)[:, None]
    sources = jnp.sum(
        matches.astype(jnp.int32) * jnp.arange(targets.shape[0], dtype=jnp.int32)[None, :], axis=1
    )
    return (sources, jnp.any(matches, axis=1))


def body(gradient, owner, stat_left, stat_right, root_left, root_right):
    groups = lax.axis_size("mp")
    ranks = lax.axis_size("dp")
    my_group = lax.axis_index("mp")
    my_rank = lax.axis_index("dp")
    my_device = my_rank * groups + my_group
    slots_own = stat_left.shape[2]
    width = gradient.shape[2]
    rows_dev = gradient.shape[1]
    table = owner.reshape(groups, groups)
    is_mine = jnp.any(table == my_device, axis=1)
    order_mine = jnp.cumsum(is_mine.astype(jnp.int32)) - 1
    slot_of_source = jnp.where(is_mine, order_mine, -1)
    slot_source, slot_live = inverse_table(slot_of_source, slots_own)
    devices = ranks * groups
    own_targets = lax.dynamic_index_in_dim(table, my_group, 0, keepdims=False)
    send_source, send_live = inverse_table(own_targets, devices)
    outgoing = select_rows(gradient, send_source, send_live)
    arrived = lax.all_to_all(outgoing, ("dp", "mp"), split_axis=0, concat_axis=0, tiled=True)
    whole = (
        arrived.reshape(ranks, groups, rows_dev, width)
        .transpose(1, 0, 2, 3)
        .reshape(groups, ranks * rows_dev, width)
    )
    blocks_in = select_rows(whole, slot_source, slot_live)
    state_shape = (slots_own, width, width)
    result, left_new, right_new, inv_left, inv_right = jax.vmap(refresh_block)(
        blocks_in,
        stat_left.reshape(state_shape),
        stat_right.reshape(state_shape),
        root_left.reshape(state_shape),
        root_right.reshape(state_shape),
    )
    live_mask = slot_live[:, None, None]
    left_new = jnp.where(live_mask, left_new, jnp.zeros_like(left_new))
    right_new = jnp.where(live_mask, right_new, jnp.zeros_like(right_new))
    inv_left = jnp.where(live_mask, inv_left, jnp.zeros_like(inv_left))
    inv_right = jnp.where(live_mask, inv_right, jnp.zeros_like(inv_right))
    spread = select_rows(result, jnp.maximum(slot_of_source, 0), is_mine)
    spread = (
        spread.reshape(groups, ranks, rows_dev, width)
        .transpose(1, 0, 2, 3)
        .reshape(devices, rows_dev, width)
    )
    returned = lax.all_to_all(spread, ("dp", "mp"), split_axis=0, concat_axis=0, tiled=True)
    final = jnp.take(returned, own_targets, axis=0)
    full_shape = stat_left.shape
    return (
        final,
        left_new.reshape(full_shape),
        right_new.reshape(full_shape),
        inv_left.reshape(full_shape),
        inv_right.reshape(full_shape),
    )


def solution(mesh):
    placed = (
        P("mp", "dp", None),
        P(),
        P("dp", "mp", None, None, None),
        P("dp", "mp", None, None, None),
        P("dp", "mp", None, None, None),
        P("dp", "mp", None, None, None),
    )
    return jax.shard_map(
        body,
        mesh=mesh,
        in_specs=placed,
        out_specs=(
            P("mp", "dp", None),
            P("dp", "mp", None, None, None),
            P("dp", "mp", None, None, None),
            P("dp", "mp", None, None, None),
            P("dp", "mp", None, None, None),
        ),
        check_vma=False,
    )
```

profile of v0, /device:TPU:1, one launch (start us, length us, event | category | flops | bytes accessed | tf_op | source)
XLA Modules:
  0.0 581.7 jit_solution(12729717403910607893)
XLA Ops:
  0.7 0.9 reshape.181
  1.8 0.5 copy-done
  2.2 7.3 %gather_fusion = f32[128,64,512]{2,1,0:T(8,128)} fusion(f32[16,64,512]{2,1,0:T(8,128)S(1)} %copy-done, s32[1024]{0:T(1024)S(1)} %pad_clamp_fusion.3), kind=kCustom, calls=%fused_computation | custom fusion | bytes 33554944 | tf_op jit(solution)/shard_map/jit(_take)/gather | solution.py:40
  9.6 12.4 %select_select_fusion = f32[128,64,512]{2,1,0:T(8,128)} fusion(f32[128,64,512]{2,1,0:T(8,128)} %gather_fusion, pred[128]{0:T(512)(128)(4,1)S(1)} %compare_and_fusion, pred[128]{0:T(512)(128)(4,1)S(1)} %fusion.45), kind=kLoop, calls=%fused_computation.6 | loop fusion | flops 8388608 | bytes 33554688 | tf_op jit(solution)/shard_map/jit(_where)/select_n | solution.py:41
  22.0 12.6 %all-to-all-start = ((f32[128,64,512]{2,1,0:T(8,128)}), f32[128,64,512]{2,1,0:T(8,128)}, u32[]{:S(2)}, u32[]{:S(2)}) async-start(f32[128,64,512]{2,1,0:T(8,128)} %select_select_fusion), calls=%async_computation | async-start | bytes 33554432 | tf_op jit(solution)/shard_map/all_to_all | solution.py:70
  35.5 1.1 fusion.43
  36.6 1.1 fusion.42
  37.7 1.0 fusion.20
  39.1 1.0 fusion.17
  40.1 6.9 %fusion.60 = f32[3,512,512]{2,1,0:T(8,128)} fusion(f32[3,512,512]{2,1,0:T(8,128)S(1)} %fusion.20), kind=kOutput, calls=%fused_computation.102 | convolution fusion | flops 4831838208 | bytes 6291456 | tf_op jit(solution)/shard_map/vmap()/dot_general | solution.py:11
  47.0 6.9 %fusion.61 = f32[3,512,512]{2,1,0:T(8,128)} fusion(f32[3,512,512]{2,1,0:T(8,128)S(1)} %fusion.17), kind=kOutput, calls=%fused_computation.103 | convolution fusion | flops 4831838208 | bytes 6291456 | tf_op jit(solution)/shard_map/vmap()/dot_general | solution.py:11
  53.9 198.4 %all-to-all-done = f32[128,64,512]{2,1,0:T(8,128)} async-done(((f32[128,64,512]{2,1,0:T(8,128)}), f32[128,64,512]{2,1,0:T(8,128)}, u32[]{:S(2)}, u32[]{:S(2)}) %all-to-all-start) | async-done | bytes 16777248 | tf_op jit(solution)/shard_map/all_to_all | solution.py:70
  252.3 12.2 %copy.44 = f32[16,8,64,512]{3,2,1,0:T(8,128)} copy(f32[16,8,64,512]{3,2,0,1:T(8,128)} %bitcast.7) | data formatting | bytes 33554432 | tf_op jit(solution)/shard_map/transpose | solution.py:73
  264.5 6.5 %gather_fusion.1 = f32[3,512,512]{2,1,0:T(8,128)S(1)} fusion(f32[16,512,512]{2,1,0:T(8,128)} %bitcast.60, s32[1024]{0:T(1024)S(1)} %pad_clamp_fusion.2), kind=kCustom, calls=%fused_computation.1 | custom fusion | bytes 6291468 | tf_op jit(solution)/shard_map/jit(_take)/gather | solution.py:40
  271.0 8.4 %bitcast_add_fusion = f32[3,512,512]{2,1,0:T(8,128)S(1)} fusion(f32[1,1,3,512,512]{4,3,2,1,0:T(8,128)} %param.9, f32[3,512,512]{2,1,0:T(8,128)S(1)} %gather_fusion.1, pred[3]{0:T(512)(128)(4,1)S(1)} %compare_and_fusion.1, pred[3]{0:T(512)(128)(4,1)S(1)} %fusion.46), kind=kOutput, calls=%fused_computation.7 | convolution fusion | flops 4834983936 | bytes 9437190 | tf_op jit(solution)/shard_map/vmap()/dot_general | solution.py:11
  279.4 6.0 %bitcast_add_fusion.1 = f32[3,512,512]{2,1,0:T(8,128)S(1)} fusion(f32[1,1,3,512,512]{4,3,2,1,0:T(8,128)S(1)} %copy-done.11, f32[3,512,512]{2,1,0:T(8,128)S(1)} %gather_fusion.1, pred[3]{0:T(512)(128)(4,1)S(1)} %compare_and_fusion.1, pred[3]{0:T(512)(128)(4,1)S(1)} %fusion.46), kind=kOutput, calls=%fused_computation.8 | convolution fusion | flops 4834983936 | bytes 9437190 | tf_op jit(solution)/shard_map/vmap()/dot_general | solution.py:11
  285.5 4.7 select_reduce_fusion
  290.2 5.8 %fusion.10 = f32[3,512,512]{2,1,0:T(8,128)S(1)} fusion(f32[3,512,512]{2,1,0:T(8,128)S(1)} %copy-done.13, f32[3,512,512]{2,1,0:T(8,128)S(1)} %bitcast_add_fusion.1, f32[512,512]{1,0:T(8,128)S(1)} %copy-done.14, f32[3]{0:T(128)S(1)} %get-tuple-element.38), kind=kOutput, calls=%fused_computation.21 | convolution fusion | flops 4833411072 | bytes 10485772 | tf_op jit(solution)/shard_map/vmap()/dot_general | solution.py:11
  296.0 5.8 %fusion.4 = f32[3,512,512]{2,1,0:T(8,128)S(1)} fusion(f32[3,512,512]{2,1,0:T(8,128)S(1)} %copy-done.12, f32[3,512,512]{2,1,0:T(8,128)S(1)} %bitcast_add_fusion, f32[3]{0:T(128)S(1)} %get-tuple-element.37, f32[512,512]{1,0:T(8,128)S(1)} %copy-done.14), kind=kOutput, calls=%fused_computation.14 | convolution fusion | flops 4833411072 | bytes 10485772 | tf_op jit(solution)/shard_map/vmap()/dot_general | solution.py:11
  301.9 5.7 fusion.1
  307.7 5.3 fusion.7
  313.0 6.3 %fusion.14 = f32[3,512,512]{2,1,0:T(8,128)S(1)} fusion(f32[3,512,512]{2,1,0:T(8,128)S(1)} %fusion.7, f32[3,512,512]{2,1,0:T(8,128)S(1)} %gather_fusion.1, pred[3]{0:T(512)(128)(4,1)S(1)} %compare_and_fusion.1, pred[3]{0:T(512)(128)(4,1)S(1)} %fusion.46), kind=kOutput, calls=%fused_computation.27 | convolution fusion | flops 4833411072 | bytes 9437190 | tf_op jit(solution)/shard_map/vmap()/dot_general | solution.py:11
  319.3 5.4 fusion.62
  324.7 7.3 %gather_fusion.2 = f32[16,512,512]{2,1,0:T(8,128)} fusion(f32[3,512,512]{2,1,0:T(8,128)S(1)} %fusion.62, s32[1024]{0:T(1024)S(1)} %pad_clamp_fusion.1), kind=kCustom, calls=%fused_computation.2 | custom fusion | bytes 33554496 | tf_op jit(solution)/shard_map/jit(_take)/gather | solution.py:40
  332.0 12.3 %fusion = f32[16,8,64,512]{3,2,0,1:T(8,128)} fusion(f32[16,8,64,512]{3,2,1,0:T(8,128)} %bitcast.59, pred[16]{0:T(512)(128)(4,1)S(1)} %get-tuple-element.31, pred[16]{0:T(512)(128)(4,1)S(1)} %compare_reduce_fusion), kind=kLoop, calls=%fused_computation.5 | loop fusion | flops 8388608 | bytes 33554464 | tf_op jit(solution)/shard_map/jit(_where)/select_n | solution.py:41
  344.3 11.0 %all-to-all-start.1 = ((f32[128,64,512]{2,1,0:T(8,128)}), f32[128,64,512]{2,1,0:T(8,128)}, u32[]{:S(2)}, u32[]{:S(2)}) async-start(f32[128,64,512]{2,1,0:T(8,128)} %bitcast.58), calls=%async_computation.1 | async-start | bytes 33554432 | tf_op jit(solution)/shard_map/all_to_all | solution.py:96
  355.5 3.9 select_bitcast_fusion.2
  359.5 2.7 copy.55
  362.2 1.6 copy.54
  363.7 206.5 %all-to-all-done.1 = f32[128,64,512]{2,1,0:T(8,128)} async-done(((f32[128,64,512]{2,1,0:T(8,128)}), f32[128,64,512]{2,1,0:T(8,128)}, u32[]{:S(2)}, u32[]{:S(2)}) %all-to-all-start.1) | async-done | bytes 16777248 | tf_op jit(solution)/shard_map/all_to_all | solution.py:96
  570.3 7.9 %gather_fusion.3 = f32[16,64,512]{2,1,0:T(8,128)} fusion(f32[128,64,512]{2,1,0:T(8,128)} %all-to-all-done.1, s32[1024]{0:T(1024)S(1)} %pad_clamp_fusion), kind=kCustom, calls=%fused_computation.3 | custom fusion | bytes 4194368 | tf_op jit(solution)/shard_map/jit(_take)/gather | solution.py:97
  578.2 3.3 broadcast_select_fusion
  (54 shorter events, 1.7 us)
Async XLA Ops:
  0.6 1.6 copy-start
  22.0 15.6 %copy-start.8 = (bf16[1,1,3,512,512]{4,3,2,1,0:T(8,128)(2,1)S(1)}, bf16[1,1,3,512,512]{4,3,2,1,0:T(8,128)(2,1)}, u32[]{:S(2)}) copy-start(bf16[1,1,3,512,512]{4,3,2,1,0:T(8,128)(2,1)} %param.10) | copy-start | bytes 4718596
  22.0 230.3 %all-to-all-start = ((f32[128,64,512]{2,1,0:T(8,128)}), f32[128,64,512]{2,1,0:T(8,128)}, u32[]{:S(2)}, u32[]{:S(2)}) async-start(f32[128,64,512]{2,1,0:T(8,128)} %select_select_fusion), calls=%async_computation | async-start | bytes 33554432 | tf_op jit(solution)/shard_map/all_to_all | solution.py:70
  37.7 1.4 copy-start.6
  271.0 8.4 %copy-start.11 = (f32[1,1,3,512,512]{4,3,2,1,0:T(8,128)S(1)}, f32[1,1,3,512,512]{4,3,2,1,0:T(8,128)}, u32[]{:S(2)}) copy-start(f32[1,1,3,512,512]{4,3,2,1,0:T(8,128)} %param.8) | copy-start | bytes 9437188
  285.5 4.7 copy-start.13
  285.5 4.7 copy-start.14
  290.2 5.8 %copy-start.12 = (f32[3,512,512]{2,1,0:T(8,128)S(1)}, f32[3,512,512]{2,1,0:T(8,128)}, u32[]{:S(2)}) copy-start(f32[3,512,512]{2,1,0:T(8,128)} %fusion.61) | copy-start | bytes 9437188
  296.0 5.9 %copy-start.5 = (f32[512,512]{1,0:T(8,128)S(1)}, f32[512,512]{1,0:T(8,128)}, u32[]{:S(2)}) copy-start(f32[512,512]{1,0:T(8,128)} %fusion.43) | copy-start | bytes 3145732
  296.0 5.9 %copy-start.7 = (bf16[1,1,3,512,512]{4,3,2,1,0:T(8,128)(2,1)S(1)}, bf16[1,1,3,512,512]{4,3,2,1,0:T(8,128)(2,1)}, u32[]{:S(2)}) copy-start(bf16[1,1,3,512,512]{4,3,2,1,0:T(8,128)(2,1)} %param.11) | copy-start | bytes 4718596
  301.9 5.8 copy-start.9
  307.7 11.6 %copy-start.4 = (f32[3,512,512]{2,1,0:T(8,128)}, f32[3,512,512]{2,1,0:T(8,128)S(1)}, u32[]{:S(2)}) copy-start(f32[3,512,512]{2,1,0:T(8,128)S(1)} %fusion.1) | copy-start | bytes 9437188
  313.0 6.3 %copy-start.2 = (f32[3,512,512]{2,1,0:T(8,128)}, f32[3,512,512]{2,1,0:T(8,128)S(1)}, u32[]{:S(2)}) copy-start(f32[3,512,512]{2,1,0:T(8,128)S(1)} %fusion.7) | copy-start | bytes 9437188
  344.3 11.2 %copy-start.3 = (f32[3,512,512]{2,1,0:T(8,128)S(1)}, f32[3,512,512]{2,1,0:T(8,128)}, u32[]{:S(2)}) copy-start(f32[3,512,512]{2,1,0:T(8,128)} %copy-done.2) | copy-start | bytes 9437188
  344.3 226.0 %all-to-all-start.1 = ((f32[128,64,512]{2,1,0:T(8,128)}), f32[128,64,512]{2,1,0:T(8,128)}, u32[]{:S(2)}, u32[]{:S(2)}) async-start(f32[128,64,512]{2,1,0:T(8,128)} %bitcast.58), calls=%async_computation.1 | async-start | bytes 33554432 | tf_op jit(solution)/shard_map/all_to_all | solution.py:96
  359.5 2.7 copy-start.10
  570.3 11.2 %copy-start.1 = (f32[16,64,512]{2,1,0:T(8,128)S(1)}, f32[16,64,512]{2,1,0:T(8,128)}, u32[]{:S(2)}) copy-start(f32[16,64,512]{2,1,0:T(8,128)} %param.6) | copy-start | bytes 6291460
where the time goes:
time: 592 us; the launch traced here: 582 us
  waiting for transfers between devices  405 us (68%)
  matrix products  64.5 us (11%)
  local copies, waits for them, and re-layouts  47.7 us (8%)
  other arithmetic  39.7 us (7%)
  starting transfers between devices  23.6 us (4%)
    all_to_all x1, waiting for transfers between devices, body(): lax.all_to_all(spread, ('dp', 'mp'), split_axis=0, concat_axis=0, tiled=T...  207 us
    all_to_all x1, waiting for transfers between devices, body(): lax.all_to_all(outgoing, ('dp', 'mp'), split_axis=0, concat_axis=0, tiled...  198 us
    dot_general x12, matrix products, matmul_high(): jnp.matmul(left_matrix, right_matrix, precision=lax.Precision.HIGHEST)  64.5 us
    select_n x2, other arithmetic, select_rows(): return jnp.where(live[:, None, None], picked, jnp.zeros_like(picked))  24.7 us
    gather x3, local copies, waits for them, and re-layouts, select_rows(): picked = jnp.take(source, index, axis=0)  21.2 us
    all_to_all x1, starting transfers between devices, body(): lax.all_to_all(outgoing, ('dp', 'mp'), split_axis=0, concat_axis=0, tiled...  12.6 us
    transpose x1, local copies, waits for them, and re-layouts, body(): whole = arrived.reshape(ranks, groups, rows_dev, width).transpose(1, 0, 2...  12.2 us
  transfers between devices with their start and end apart: 2, of which 2 were waited for; matrix products, arithmetic and copies ran while one was open for 5% of the time, Pallas kernels for 0%

commit v1 on v0

v1 whole, which is shorter than its diff:
```python
import functools

import jax
import jax.numpy as jnp
from jax import lax
from jax.experimental import pallas as pl
from jax.experimental.pallas import tpu as pltpu
from jax.sharding import PartitionSpec as P

MESH = pl.DeviceIdType.MESH
N = 512
ROWS = 64
OWN = 3
RANKS = 8
GROUPS = 16
SIDE = 4
GATHER = ((0, 16), (16, 16), (32, 16), (48, 16))
RETURN = ((0, 16), (16, 16), (32, 16), (48, 16))
LATE = 2
TINY = 2.0**-48

SEND1, SLOT2, SLOT3, ORDER4, LIVE = 0, 16, 40, 56, 72


def tables(owner, group, rank):
    table = owner.reshape(GROUPS, GROUPS)
    of_group, of_rank = table % GROUPS, table // GROUPS
    each = jnp.arange(GROUPS, dtype=jnp.int32)

    def away(target, source):
        dz = (target // SIDE - source // SIDE) % SIDE
        dy = (target % SIDE - source % SIDE) % SIDE
        return dz * SIDE + dy

    mine = lax.dynamic_index_in_dim(of_group, group, 0, keepdims=False)
    sent_to = away(mine, group)
    send1 = jnp.sum(jnp.where(sent_to[None, :] == each[:, None], each[None, :], 0), axis=1)
    rank_of = jnp.sum(jnp.where(of_group == group, of_rank, 0), axis=1)
    before = (rank_of[:, None] == rank_of[None, :]) & (each[:, None] > each[None, :])
    slot_of = jnp.sum(before.astype(jnp.int32), axis=1)
    place = rank_of * OWN + slot_of
    came = away(group, each)
    places = jnp.arange(RANKS * OWN, dtype=jnp.int32)
    hit = place[None, :] == places[:, None]
    slot2 = jnp.sum(jnp.where(hit, came[None, :], 0), axis=1)
    goes = away(each, group)
    back = slot_of * RANKS + rank_of
    slot3 = jnp.sum(jnp.where(goes[None, :] == each[:, None], back[None, :], 0), axis=1)
    order4 = away(group, mine)
    slots = jnp.arange(OWN, dtype=jnp.int32)
    live = jnp.any(place[None, :] == (rank * OWN + slots)[:, None], axis=1).astype(jnp.int32)
    return jnp.concatenate([send1, slot2, slot3, order4, live]).astype(jnp.int32)


def split(x):
    high = x.astype(jnp.bfloat16)
    return high, (x - high.astype(jnp.float32)).astype(jnp.bfloat16)


def dot(a, b):
    return jnp.dot(a, b, preferred_element_type=jnp.float32)


def dot3(a, b):
    (ah, al), (bh, bl) = a, b
    return dot(ah, bh) + (dot(ah, bl) + dot(al, bh))


def kernel(tab, grad, stat_l, stat_r, root_l, root_r, out, new_sl, new_sr, new_rl, new_rr, *scratch):
    ng, nr = len(GATHER), len(RETURN)
    scratch = list(scratch)
    take = lambda count: [scratch.pop(0) for _ in range(count)]
    staged, recv1, recv3, recv4 = take(ng), take(ng), take(nr), take(nr)
    send1, send2, gbuf, send3, send4, outv, st, rt, x5 = take(9)
    in_sem, out_sem, s1, r1, s2, r2, s3, r3, s4, r4 = take(10)

    rank, group = lax.axis_index("dp"), lax.axis_index("mp")
    z, y = group // SIDE, group % SIDE

    def mp_peer(k):
        return (rank, ((z + k // SIDE) % SIDE) * SIDE + (y + k % SIDE) % SIDE)

    def dp_peer(d):
        return ((rank + d) % RANKS, group)

    def remote(src, dst, ssem, rsem, peer):
        return pltpu.make_async_remote_copy(
            src_ref=src, dst_ref=dst, send_sem=ssem, recv_sem=rsem, device_id=peer, device_id_type=MESH
        )

    def wait_recv(region, sem):
        remote(region, region, s1, sem, dp_peer(1)).wait_recv()

    def wait_send(region, sem):
        remote(region, region, sem, r1.at[0], dp_peer(1)).wait_send()

    grad_in = [
        pltpu.make_async_copy(grad.at[:, pl.ds(a, n), :], staged[i], in_sem.at[i]) for i, (a, n) in enumerate(GATHER)
    ]
    state_in = [
        pltpu.make_async_copy(src.at[0, 0], dst, in_sem.at[ng + i])
        for i, (src, dst) in enumerate(
            ((root_l, rt.at[0]), (root_r, rt.at[1]), (stat_l, st.at[0]), (stat_r, st.at[1]))
        )
    ]
    for copy in grad_in + state_in:
        copy.start()

    barrier = pltpu.get_barrier_semaphore()

    def greet_mp(k, carry):
        pl.semaphore_signal(barrier, inc=1, device_id=mp_peer(k), device_id_type=MESH)
        return carry

    def greet_dp(d, carry):
        pl.semaphore_signal(barrier, inc=1, device_id=dp_peer(d), device_id_type=MESH)
        return carry

    lax.fori_loop(1, GROUPS, greet_mp, 0)
    lax.fori_loop(1, RANKS, greet_dp, 0)
    pl.semaphore_wait(barrier, GROUPS - 1 + RANKS - 1)

    for i, (a, n) in enumerate(GATHER):
        grad_in[i].wait()
        rows = pl.ds(a, n)
        recv1[i][0] = staged[i][tab[SEND1]]

        def step1(k, carry, i=i, rows=rows):
            send1[k, rows, :] = staged[i][tab[SEND1 + k]]
            remote(send1.at[k, rows], recv1[i].at[k], s1, r1.at[i], mp_peer(k)).start()
            return carry

        lax.fori_loop(1, GROUPS, step1, 0)

    def second(i, slots, fill):
        a, n = GATHER[i]
        rows = pl.ds(a, n)

        def step2(d, carry):
            peer = (rank + d) % RANKS
            for s in slots:
                if fill:
                    send2[d * OWN + s, rows, :] = recv1[i][tab[SLOT2 + peer * OWN + s]]
                remote(send2.at[d * OWN + s, rows], gbuf.at[s, rank, rows], s2, r2.at[s], dp_peer(d)).start()
            return carry

        lax.fori_loop(1, RANKS, step2, 0)

    def own_rows(i):
        a, n = GATHER[i]
        for s in range(OWN):
            gbuf[s, rank, pl.ds(a, n), :] = recv1[i][tab[SLOT2 + rank * OWN + s]]

    def power(t, carry):
        side, s = t // OWN, t % OWN
        x = rt[side, s]
        sq = split(dot(x, x))
        fourth = split(dot3(sq, sq) * TINY)
        high, low = split(dot(x, fourth[0]) + dot(x, fourth[1]))
        x5[side, s, 0] = high
        x5[side, s, 1] = low
        return carry

    units = 2 * OWN
    for i, (a, n) in enumerate(GATHER):
        wait_recv(recv1[i].at[pl.ds(1, GROUPS - 1)], r1.at[i])
        second(i, (0, 1, 2) if i < LATE else (0, 1), True)
        if i == ng - 1:
            for late in range(LATE, ng):
                second(late, (2,), True)
        own_rows(i)
        if i == 0:
            state_in[0].wait()
            state_in[1].wait()
        first, last = units * i // (ng - 1), units * (i + 1) // (ng - 1)
        if i < ng - 1:
            lax.fori_loop(first, last, power, 0)
    state_in[2].wait()
    state_in[3].wait()

    eye = lax.broadcasted_iota(jnp.int32, (N, N), 0) == lax.broadcasted_iota(jnp.int32, (N, N), 1)

    def newton(side, s, new, taken):
        scale = jnp.sum(jnp.where(eye, new, 0.0)) / N
        shifted = split(new / scale + jnp.where(eye, 0.001, 0.0))
        moved = dot3((x5[side, s, 0], x5[side, s, 1]), shifted)
        inverse = 1.25 * rt[side, s].astype(jnp.float32) - (0.25 / TINY) * moved
        st[side, s] = jnp.where(taken, new, 0.0)
        rt[side, s] = jnp.where(taken, inverse, 0.0).astype(jnp.bfloat16)
        return inverse

    def refresh(s, carry):
        wait_recv(gbuf.at[s, pl.ds(0, RANKS - 1)], r2.at[s])
        taken = tab[LIVE + s] > 0
        g32 = gbuf[s].reshape(N, N)
        g, gt = split(g32), split(g32.T)
        inv_l = newton(0, s, 0.95 * st[0, s] + dot3(g, gt), taken)
        inv_r = newton(1, s, 0.95 * st[1, s] + dot3(gt, g), taken)
        result = dot3(split(dot3(split(inv_l), g)), split(inv_r))
        send3[pl.ds(s * RANKS, RANKS)] = result.reshape(RANKS, ROWS, N)
        for i, (a, n) in enumerate(RETURN):
            rows = pl.ds(a, n)

            def step3(d, carry, i=i, rows=rows):
                peer = (rank + d) % RANKS
                remote(
                    send3.at[s * RANKS + peer, rows], recv3[i].at[s * RANKS + rank], s3, r3.at[i], dp_peer(d)
                ).start()
                return carry

            lax.fori_loop(1, RANKS, step3, 0)
            recv3[i][s * RANKS + rank] = send3[s * RANKS + rank, rows, :]
        for side, (stat, root) in enumerate(((new_sl, new_rl), (new_sr, new_rr))):
            pltpu.make_async_copy(st.at[side, s], stat.at[0, 0, s], out_sem.at[0, side, s]).start()
            pltpu.make_async_copy(rt.at[side, s], root.at[0, 0, s], out_sem.at[1, side, s]).start()
        return carry

    lax.fori_loop(0, OWN, refresh, 0)

    for i, (a, n) in enumerate(RETURN):
        rows = pl.ds(a, n)
        wait_recv(recv3[i].at[pl.ds(0, OWN * (RANKS - 1))], r3.at[i])
        recv4[i][0] = recv3[i][tab[SLOT3]]

        def step4(k, carry, i=i, rows=rows):
            send4[k, rows, :] = recv3[i][tab[SLOT3 + k]]
            remote(send4.at[k, rows], recv4[i].at[k], s4, r4.at[i], mp_peer(k)).start()
            return carry

        lax.fori_loop(1, GROUPS, step4, 0)

    final = []
    for i, (a, n) in enumerate(RETURN):
        rows = pl.ds(a, n)
        wait_recv(recv4[i].at[pl.ds(1, GROUPS - 1)], r4.at[i])

        def step5(j, carry, i=i, rows=rows):
            outv[j, rows, :] = recv4[i][tab[ORDER4 + j]]
            return carry

        lax.fori_loop(0, GROUPS, step5, 0)
        final.append(pltpu.make_async_copy(outv.at[:, rows, :], out.at[:, rows, :], in_sem.at[i]))
        final[-1].start()

    for s in range(OWN):
        for side, (stat, root) in enumerate(((new_sl, new_rl), (new_sr, new_rr))):
            pltpu.make_async_copy(st.at[side, s], stat.at[0, 0, s], out_sem.at[0, side, s]).wait()
            pltpu.make_async_copy(rt.at[side, s], root.at[0, 0, s], out_sem.at[1, side, s]).wait()
    wait_send(send1.at[pl.ds(1, GROUPS - 1)], s1)
    wait_send(send2.at[pl.ds(0, OWN * (RANKS - 1))], s2)
    wait_send(send3.at[pl.ds(0, OWN * (RANKS - 1))], s3)
    wait_send(send4.at[pl.ds(1, GROUPS - 1)], s4)
    for copy in final:
        copy.wait()


def body(gradient, owner, stat_left, stat_right, root_left, root_right):
    group, rank = lax.axis_index("mp"), lax.axis_index("dp")
    tab = tables(owner, group, rank)
    f32, bf16 = jnp.float32, jnp.bfloat16
    ng, nr = len(GATHER), len(RETURN)
    vmem, dma = pltpu.VMEM, pltpu.SemaphoreType.DMA
    anywhere = pl.BlockSpec(memory_space=pl.ANY)
    scratch = (
        [vmem((GROUPS, n, N), f32) for _, n in GATHER]
        + [vmem((GROUPS, n, N), f32) for _, n in GATHER]
        + [vmem((OWN * RANKS, n, N), f32) for _, n in RETURN]
        + [vmem((GROUPS, n, N), f32) for _, n in RETURN]
        + [
            vmem((GROUPS, ROWS, N), f32),
            vmem((OWN * RANKS, ROWS, N), f32),
            vmem((OWN, RANKS, ROWS, N), f32),
            vmem((OWN * RANKS, ROWS, N), f32),
            vmem((GROUPS, ROWS, N), f32),
            vmem((GROUPS, ROWS, N), f32),
            vmem((2, OWN, N, N), f32),
            vmem((2, OWN, N, N), bf16),
            vmem((2, OWN, 2, N, N), bf16),
        ]
        + [
            dma((max(ng + 4, nr),)),
            dma((2, 2, OWN)),
            dma,
            dma((ng,)),
            dma,
            dma((OWN,)),
            dma,
            dma((nr,)),
            dma,
            dma((nr,)),
        ]
    )
    shape = jax.ShapeDtypeStruct
    return pl.pallas_call(
        kernel,
        out_shape=(
            shape(gradient.shape, f32),
            shape(stat_left.shape, f32),
            shape(stat_right.shape, f32),
            shape(root_left.shape, bf16),
            shape(root_right.shape, bf16),
        ),
        in_specs=[pl.BlockSpec(memory_space=pltpu.SMEM)] + [anywhere] * 5,
        out_specs=(anywhere,) * 5,
        scratch_shapes=scratch,
        compiler_params=pltpu.CompilerParams(
            collective_id=0, has_side_effects=True, vmem_limit_bytes=60 * 2**20
        ),
        cost_estimate=pl.CostEstimate(flops=75 * 2 * N**3, bytes_accessed=22 * 2**20, transcendentals=0),
        name="refresh",
    )(tab, gradient, stat_left, stat_right, root_left, root_right)


def solution(mesh):
    state = P("dp", "mp", None, None, None)
    return jax.shard_map(
        body,
        mesh=mesh,
        in_specs=(P("mp", "dp", None), P(), state, state, state, state),
        out_specs=(P("mp", "dp", None), state, state, state, state),
        check_vma=False,
    )
```

time: 592 us -> 126 us (0.21); the launches traced: 582 us -> 125 us
  waiting for transfers between devices: 405 us -> 0 us
  Pallas kernels: 0 us -> 111 us
  matrix products: 64.5 us -> 0 us
  other arithmetic: 39.7 us -> 0.89 us
  local copies, waits for them, and re-layouts: 47.7 us -> 13.3 us
  starting transfers between devices: 23.6 us -> 0 us
    all_to_all x2 -> x0, waiting for transfers between devices: 405 us -> none  [the longest x1 207 us: body(): lax.all_to_all(spread, ('dp', 'mp'), split_axis=0, concat_axis=0, tiled=T...]
    pallas_call x0 -> x1, Pallas kernels: none -> 111 us  [body(): pl.pallas_call(kernel, out_shape=(shape(gradient.shape, f32), shape(stat_...]
    dot_general x12 -> x0, matrix products: 64.5 us -> none  [matmul_high(): jnp.matmul(left_matrix, right_matrix, precision=lax.Precision.HIGHEST)]
    gather x4 -> x0, local copies, waits for them, and re-layouts: 29.1 us -> none  [the longest x3 21.2 us: select_rows(): picked = jnp.take(source, index, axis=0)]
    select_n x6 -> x0, other arithmetic: 28.1 us -> none  [the longest x2 24.7 us: select_rows(): return jnp.where(live[:, None, None], picked, jnp.zeros_like(picked))]
    all_to_all x2 -> x0, starting transfers between devices: 23.6 us -> none  [the longest x1 12.6 us: body(): lax.all_to_all(outgoing, ('dp', 'mp'), split_axis=0, concat_axis=0, tiled...]
    transpose x1 -> x0, local copies, waits for them, and re-layouts: 12.2 us -> none  [body(): whole = arrived.reshape(ranks, groups, rows_dev, width).transpose(1, 0, 2...]
    unnamed x32 -> x13, local copies, waits for them, and re-layouts: 5.22 us -> 12 us
  transfers between devices with their start and end apart: 2 -> 0, of which waited for: 2 -> 0; matrix products, arithmetic and copies ran while one was open for 5% -> 0% of each run, Pallas kernels for 0% -> 0%
where the time goes in v1:
time: 126 us; the launch traced here: 125 us
  Pallas kernels  111 us (88%)
  local copies, waits for them, and re-layouts  13.3 us (11%)
    pallas_call x1, Pallas kernels, body(): pl.pallas_call(kernel, out_shape=(shape(gradient.shape, f32), shape(stat_...  111 us
    unnamed x13, local copies, waits for them, and re-layouts  12 us

profile of v1, /device:TPU:1, one launch (start us, length us, event | category | flops | bytes accessed | tf_op | source)
XLA Modules:
  0.0 125.5 jit_solution(16269269186916968271)
XLA Ops:
  0.7 0.8 reshape.105
  1.4 0.1 fusion.1
  1.6 0.2 convert_reduce_fusion
  1.8 0.2 compare_reduce_fusion
  2.0 0.1 select_reduce_fusion.1
  2.1 0.1 select_reduce_fusion
  2.2 0.1 select_reduce_fusion.2
  2.3 0.6 concatenate.3.tab
  2.9 110.5 %refresh.1 = (f32[16,64,512]{2,1,0:T(8,128)}, f32[1,1,3,512,512]{4,3,2,1,0:T(8,128)}, f32[1,1,3,512,512]{4,3,2,1,0:T(8,128)}, bf16[1,1,3,512,512]{4,3,2,1,0:T(8,128)(2,1)}, bf16[1,1,3,512,512]{4,3,2,1,0:T(8,128)(2,1)}) custom-call(s32[75]{0:T(128)} %concatenate.3.tab, f32[16,64,512]{2,1,0:T(8,128)} %grad.1, f32[1,1,3,512,512]{4,3,2,1,0:T(8,128)} %stat_l.1, ...), custom_call_target="tpu_custom_call" | custom-call | flops 20132659200 | bytes 23068672 | tf_op jit(solution)/shard_map/refresh/pallas_call | solution.py:294
  113.5 0.0 copy-start.1
  113.5 3.3 %copy.16 = f32[16,64,512]{2,1,0:T(8,128)} copy(f32[16,64,512]{2,1,0:T(8,128)} %get-tuple-element.17) | data formatting | bytes 4194304
  116.8 0.0 copy-done.1
  116.8 0.0 copy-start
  116.8 1.7 %copy.17 = f32[1,1,3,512,512]{4,3,2,1,0:T(8,128)} copy(f32[1,1,3,512,512]{4,3,2,1,0:T(8,128)S(1)} %copy-done.1) | data formatting | bytes 6291456
  118.4 1.4 %copy-done = f32[1,1,3,512,512]{4,3,2,1,0:T(8,128)S(1)} copy-done((f32[1,1,3,512,512]{4,3,2,1,0:T(8,128)S(1)}, f32[1,1,3,512,512]{4,3,2,1,0:T(8,128)}, u32[]{:S(2)}) %copy-start) | copy-done | bytes 3145752
  119.8 0.0 copy-start.3
  119.8 1.7 %copy.18 = f32[1,1,3,512,512]{4,3,2,1,0:T(8,128)} copy(f32[1,1,3,512,512]{4,3,2,1,0:T(8,128)S(1)} %copy-done) | data formatting | bytes 6291456
  121.5 0.9 copy-done.3
  122.4 0.0 copy-start.2
  122.4 1.1 copy.19
  123.5 0.8 copy-done.2
  124.3 1.1 copy.20
  (5 shorter events, 0.1 us)
Async XLA Ops:
  113.5 3.3 %copy-start.1 = (f32[1,1,3,512,512]{4,3,2,1,0:T(8,128)S(1)}, f32[1,1,3,512,512]{4,3,2,1,0:T(8,128)}, u32[]{:S(2)}) copy-start(f32[1,1,3,512,512]{4,3,2,1,0:T(8,128)} %get-tuple-element.18) | copy-start | bytes 9437188
  116.8 3.0 %copy-start = (f32[1,1,3,512,512]{4,3,2,1,0:T(8,128)S(1)}, f32[1,1,3,512,512]{4,3,2,1,0:T(8,128)}, u32[]{:S(2)}) copy-start(f32[1,1,3,512,512]{4,3,2,1,0:T(8,128)} %get-tuple-element.19) | copy-start | bytes 9437188
  119.8 2.5 %copy-start.3 = (bf16[1,1,3,512,512]{4,3,2,1,0:T(8,128)(2,1)S(1)}, bf16[1,1,3,512,512]{4,3,2,1,0:T(8,128)(2,1)}, u32[]{:S(2)}) copy-start(bf16[1,1,3,512,512]{4,3,2,1,0:T(8,128)(2,1)} %get-tuple-element.20) | copy-start | bytes 4718596
  122.4 2.0 %copy-start.2 = (bf16[1,1,3,512,512]{4,3,2,1,0:T(8,128)(2,1)S(1)}, bf16[1,1,3,512,512]{4,3,2,1,0:T(8,128)(2,1)}, u32[]{:S(2)}) copy-start(bf16[1,1,3,512,512]{4,3,2,1,0:T(8,128)(2,1)} %get-tuple-element.21) | copy-start | bytes 4718596

commit v2 on v1

v2 whole, which is shorter than its diff:
```python
import functools

import jax
import jax.numpy as jnp
from jax import lax
from jax.experimental import pallas as pl
from jax.experimental.pallas import tpu as pltpu
from jax.sharding import PartitionSpec as P

MESH = pl.DeviceIdType.MESH
N = 512
ROWS = 64
OWN = 3
RANKS = 8
GROUPS = 16
SIDE = 4
GATHER = ((0, 8), (8, 8), (16, 8), (24, 8), (32, 16), (48, 16))
RETURN = ((0, 16), (16, 16), (32, 16), (48, 8), (56, 8))
LATE = 4
EARLY = 2
TINY = 2.0**-48

SEND1, SLOT2, SLOT3, RANK3, ORDER4, LIVE = 0, 16, 40, 56, 72, 88


def tables(owner, group, rank):
    table = owner.reshape(GROUPS, GROUPS)
    of_group, of_rank = table % GROUPS, table // GROUPS
    each = jnp.arange(GROUPS, dtype=jnp.int32)

    def away(target, source):
        dz = (target // SIDE - source // SIDE) % SIDE
        dy = (target % SIDE - source % SIDE) % SIDE
        return dz * SIDE + dy

    mine = lax.dynamic_index_in_dim(of_group, group, 0, keepdims=False)
    sent_to = away(mine, group)
    send1 = jnp.sum(jnp.where(sent_to[None, :] == each[:, None], each[None, :], 0), axis=1)
    rank_of = jnp.sum(jnp.where(of_group == group, of_rank, 0), axis=1)
    before = (rank_of[:, None] == rank_of[None, :]) & (each[:, None] > each[None, :])
    slot_of = jnp.sum(before.astype(jnp.int32), axis=1)
    place = rank_of * OWN + slot_of
    came = away(group, each)
    places = jnp.arange(RANKS * OWN, dtype=jnp.int32)
    hit = place[None, :] == places[:, None]
    slot2 = jnp.sum(jnp.where(hit, came[None, :], 0), axis=1)
    goes = away(each, group)
    met = goes[None, :] == each[:, None]
    slot3 = jnp.sum(jnp.where(met, slot_of[None, :], 0), axis=1)
    rank3 = jnp.sum(jnp.where(met, rank_of[None, :], 0), axis=1)
    order4 = away(group, mine)
    slots = jnp.arange(OWN, dtype=jnp.int32)
    live = jnp.any(place[None, :] == (rank * OWN + slots)[:, None], axis=1).astype(jnp.int32)
    return jnp.concatenate([send1, slot2, slot3, rank3, order4, live]).astype(jnp.int32)


def split(x):
    high = x.astype(jnp.bfloat16)
    return high, (x - high.astype(jnp.float32)).astype(jnp.bfloat16)


def dot(a, b):
    return jnp.dot(a, b, preferred_element_type=jnp.float32)


def dot3(a, b):
    (ah, al), (bh, bl) = a, b
    return dot(ah, bh) + (dot(ah, bl) + dot(al, bh))


def kernel(tab, grad, stat_l, stat_r, root_l, root_r, outv, new_sl, new_sr, new_rl, new_rr, *scratch):
    ng, nr = len(GATHER), len(RETURN)
    scratch = list(scratch)
    take = lambda count: [scratch.pop(0) for _ in range(count)]
    staged, recv1, recv3, recv4 = take(ng), take(ng), take(nr), take(nr)
    send1, send2, gbuf, send3, send4, x5 = take(6)
    in_sem, s1, r1, s2, r2, s3, r3, s4, r4 = take(9)

    st, rt = (new_sl.at[0, 0], new_sr.at[0, 0]), (new_rl.at[0, 0], new_rr.at[0, 0])
    rank, group = lax.axis_index("dp"), lax.axis_index("mp")
    z, y = group // SIDE, group % SIDE

    def mp_peer(k):
        return (rank, ((z + k // SIDE) % SIDE) * SIDE + (y + k % SIDE) % SIDE)

    def dp_peer(d):
        return ((rank + d) % RANKS, group)

    def remote(src, dst, ssem, rsem, peer):
        return pltpu.make_async_remote_copy(
            src_ref=src, dst_ref=dst, send_sem=ssem, recv_sem=rsem, device_id=peer, device_id_type=MESH
        )

    def wait_recv(region, sem):
        remote(region, region, s1, sem, dp_peer(1)).wait_recv()

    def wait_send(region, sem):
        remote(region, region, sem, r1.at[0], dp_peer(1)).wait_send()

    grad_in = [
        pltpu.make_async_copy(grad.at[:, pl.ds(a, n), :], staged[i], in_sem.at[i]) for i, (a, n) in enumerate(GATHER)
    ]
    state_in = [
        pltpu.make_async_copy(src.at[0, 0], dst, in_sem.at[ng + i])
        for i, (src, dst) in enumerate(
            ((root_l, rt[0]), (root_r, rt[1]), (stat_l, st[0]), (stat_r, st[1]))
        )
    ]
    for copy in grad_in + state_in:
        copy.start()

    barrier = pltpu.get_barrier_semaphore()

    def greet_mp(k, carry):
        pl.semaphore_signal(barrier, inc=1, device_id=mp_peer(k), device_id_type=MESH)
        return carry

    def greet_dp(d, carry):
        pl.semaphore_signal(barrier, inc=1, device_id=dp_peer(d), device_id_type=MESH)
        return carry

    lax.fori_loop(1, GROUPS, greet_mp, 0)
    lax.fori_loop(1, RANKS, greet_dp, 0)
    pl.semaphore_wait(barrier, GROUPS - 1 + RANKS - 1)

    for i, (a, n) in enumerate(GATHER):
        grad_in[i].wait()
        rows = pl.ds(a, n)
        recv1[i][0] = staged[i][tab[SEND1]]

        def step1(k, carry, i=i, rows=rows):
            send1[k, rows, :] = staged[i][tab[SEND1 + k]]
            remote(send1.at[k, rows], recv1[i].at[k], s1, r1.at[i], mp_peer(k)).start()
            return carry

        lax.fori_loop(1, GROUPS, step1, 0)

    def second(i, slots):
        rows = pl.ds(*GATHER[i])

        def fill(d, carry):
            peer = (rank + d) % RANKS
            for s in range(OWN):
                send2[d, s, rows, :] = recv1[i][tab[SLOT2 + peer * OWN + s]]
            return carry

        def step2(d, carry):
            fill(d, carry)
            leave(d, slots, rows, 0 if slots == OWN else 1)
            return carry

        lax.fori_loop(1, RANKS, step2, 0)

    def leave(d, slots, rows, sem):
        some = pl.ds(0, slots)
        remote(send2.at[d, some, rows], gbuf.at[some, rank, rows], s2, r2.at[sem], dp_peer(d)).start()

    late_from = GATHER[LATE][0]
    late_rows = pl.ds(late_from, ROWS - late_from)

    def step2_late(d, carry):
        some = pl.ds(OWN - 1, 1)
        remote(send2.at[d, some, late_rows], gbuf.at[some, rank, late_rows], s2, r2.at[2], dp_peer(d)).start()
        return carry

    def own_rows(i):
        a, n = GATHER[i]
        for s in range(OWN):
            gbuf[s, rank, pl.ds(a, n), :] = recv1[i][tab[SLOT2 + rank * OWN + s]]

    def power(t):
        side = t % 2
        s = t // 2
        x = rt[side][s]
        sq = split(dot(x, x))
        fourth = split(dot3(sq, sq) * TINY)
        high, low = split(dot(x, fourth[0]) + dot(x, fourth[1]))
        x5[side, s, 0] = high
        x5[side, s, 1] = low

    for i in range(ng):
        wait_recv(recv1[i].at[pl.ds(1, GROUPS - 1)], r1.at[i])
        second(i, OWN if i < LATE else OWN - 1)
        if i == ng - 1:
            lax.fori_loop(1, RANKS, step2_late, 0)
        own_rows(i)
        if i == 0:
            state_in[0].wait()
            state_in[1].wait()
        power(i)
    state_in[2].wait()
    state_in[3].wait()

    eye = lax.broadcasted_iota(jnp.int32, (N, N), 0) == lax.broadcasted_iota(jnp.int32, (N, N), 1)

    def newton(side, s, new, taken):
        scale = jnp.sum(jnp.where(eye, new, 0.0)) / N
        shifted = split(new / scale + jnp.where(eye, 0.001, 0.0))
        moved = dot3((x5[side, s, 0], x5[side, s, 1]), shifted)
        inverse = 1.25 * rt[side][s].astype(jnp.float32) - (0.25 / TINY) * moved
        st[side][s] = jnp.where(taken, new, 0.0)
        rt[side][s] = jnp.where(taken, inverse, 0.0).astype(jnp.bfloat16)
        return inverse

    def refresh(s):
        taken = tab[LIVE + s] > 0
        g32 = gbuf[s].reshape(N, N)
        g, gt = split(g32), split(g32.T)
        inv_l = newton(0, s, 0.95 * st[0][s] + dot3(g, gt), taken)
        inv_r = newton(1, s, 0.95 * st[1][s] + dot3(gt, g), taken)
        result = dot3(split(dot3(split(inv_l), g)), split(inv_r))
        send3[s] = result.reshape(RANKS, ROWS, N)

    def back(i, first, count):
        rows, some = pl.ds(*RETURN[i]), pl.ds(first, count)

        def step3(d, carry):
            peer = (rank + d) % RANKS
            remote(send3.at[some, peer, rows], recv3[i].at[some, rank], s3, r3.at[i], dp_peer(d)).start()
            return carry

        lax.fori_loop(1, RANKS, step3, 0)
        for s in range(first, first + count):
            recv3[i][s, rank] = send3[s, rank, rows, :]

    early = pl.ds(0, late_from)
    wait_recv(gbuf.at[:, pl.ds(0, RANKS - 1), early], r2.at[0])
    wait_recv(gbuf.at[pl.ds(0, OWN - 1), pl.ds(0, RANKS - 1), late_rows], r2.at[1])
    refresh(0)
    for i in range(EARLY):
        back(i, 0, 1)
    lax.fori_loop(1, OWN - 1, lambda s, carry: (refresh(s), carry)[1], 0)
    wait_recv(gbuf.at[pl.ds(OWN - 1, 1), pl.ds(0, RANKS - 1), late_rows], r2.at[2])
    refresh(OWN - 1)
    for i in range(nr):
        back(i, *((1, OWN - 1) if i < EARLY else (0, OWN)))

    for i, (a, n) in enumerate(RETURN):
        rows = pl.ds(a, n)
        wait_recv(recv3[i].at[:, pl.ds(0, RANKS - 1)], r3.at[i])

        def pick(k, i=i):
            return recv3[i][tab[SLOT3 + k], tab[RANK3 + k]]

        recv4[i][0] = pick(0)

        def step4(k, carry, i=i, rows=rows, pick=pick):
            send4[k, rows, :] = pick(k)
            remote(send4.at[k, rows], recv4[i].at[k], s4, r4.at[i], mp_peer(k)).start()
            return carry

        lax.fori_loop(1, GROUPS, step4, 0)

    for i, (a, n) in enumerate(RETURN):
        rows = pl.ds(a, n)
        wait_recv(recv4[i].at[pl.ds(1, GROUPS - 1)], r4.at[i])

        def step5(j, carry, i=i, rows=rows):
            outv[j, rows, :] = recv4[i][tab[ORDER4 + j]]
            return carry

        lax.fori_loop(0, GROUPS, step5, 0)

    wait_send(send1.at[pl.ds(1, GROUPS - 1)], s1)
    wait_send(send2.at[pl.ds(1, RANKS - 1)], s2)
    wait_send(send3.at[:, pl.ds(0, RANKS - 1)], s3)
    wait_send(send4.at[pl.ds(1, GROUPS - 1)], s4)


def finish(*refs):
    count = len(refs) // 2
    copies = [pltpu.make_async_copy(refs[i], refs[count + i], refs[-1].at[i]) for i in range(count)]
    for copy in copies:
        copy.start()
    for copy in copies:
        copy.wait()


def body(gradient, owner, stat_left, stat_right, root_left, root_right):
    group, rank = lax.axis_index("mp"), lax.axis_index("dp")
    tab = tables(owner, group, rank)
    f32, bf16 = jnp.float32, jnp.bfloat16
    ng, nr = len(GATHER), len(RETURN)
    vmem, dma = pltpu.VMEM, pltpu.SemaphoreType.DMA
    anywhere = pl.BlockSpec(memory_space=pl.ANY)
    scratch = (
        [vmem((GROUPS, n, N), f32) for _, n in GATHER]
        + [vmem((GROUPS, n, N), f32) for _, n in GATHER]
        + [vmem((OWN, RANKS, n, N), f32) for _, n in RETURN]
        + [vmem((GROUPS, n, N), f32) for _, n in RETURN]
        + [
            vmem((GROUPS, ROWS, N), f32),
            vmem((RANKS, OWN, ROWS, N), f32),
            vmem((OWN, RANKS, ROWS, N), f32),
            vmem((OWN, RANKS, ROWS, N), f32),
            vmem((GROUPS, ROWS, N), f32),
            vmem((2, OWN, 2, N, N), bf16),
        ]
        + [dma((ng + 4,)), dma, dma((ng,)), dma, dma((3,)), dma, dma((nr,)), dma, dma((nr,))]
    )
    args = (gradient, stat_left, stat_right, root_left, root_right)
    results = pl.pallas_call(
        kernel,
        out_shape=tuple(pltpu.VMEM(x.shape, x.dtype) for x in args),
        in_specs=[pl.BlockSpec(memory_space=pltpu.SMEM)] + [anywhere] * 5,
        out_specs=(pl.BlockSpec(memory_space=pltpu.VMEM),) * 5,
        scratch_shapes=scratch,
        compiler_params=pltpu.CompilerParams(
            collective_id=0, has_side_effects=True, vmem_limit_bytes=48 * 2**20
        ),
        cost_estimate=pl.CostEstimate(flops=75 * 2 * N**3, bytes_accessed=22 * 2**20, transcendentals=0),
        name="refresh",
    )(tab, *args)
    return pl.pallas_call(
        finish,
        out_shape=tuple(jax.ShapeDtypeStruct(x.shape, x.dtype) for x in args),
        in_specs=[anywhere] * 5,
        out_specs=(anywhere,) * 5,
        scratch_shapes=[dma((5,))],
        name="finish",
    )(*results)


def solution(mesh):
    state = P("dp", "mp", None, None, None)
    return jax.shard_map(
        body,
        mesh=mesh,
        in_specs=(P("mp", "dp", None), P(), state, state, state, state),
        out_specs=(P("mp", "dp", None), state, state, state, state),
        check_vma=False,
    )
```

time: 126 us -> 463 us (3.67)
  Pallas kernels: 111 us -> 453 us
  local copies, waits for them, and re-layouts: 13.3 us -> 8.44 us
    pallas_call x1 -> x2, Pallas kernels: 111 us -> 453 us  [the longest x1 351 us: body(): pl.pallas_call(finish, out_shape=tuple((jax.ShapeDtypeStruct(x.shape, x.d...]
    unnamed x13 -> x10, local copies, waits for them, and re-layouts: 12 us -> 7.08 us
where the time goes in v2:
time: 463 us
  Pallas kernels  453 us (98%)
  local copies, waits for them, and re-layouts  8.44 us (2%)
    pallas_call x1, Pallas kernels, body(): pl.pallas_call(finish, out_shape=tuple((jax.ShapeDtypeStruct(x.shape, x.d...  351 us
    pallas_call x1, Pallas kernels, body(): pl.pallas_call(kernel, out_shape=tuple((pltpu.VMEM(x.shape, x.dtype) for...  102 us

profile of v2, /device:TPU:1, one launch (start us, length us, event | category | flops | bytes accessed | tf_op | source)
XLA Modules:
  0.0 462.8 jit_solution(7635710381916385110)
XLA Ops:
  0.7 0.8 reshape.100
  1.4 0.1 fusion.1
  1.6 0.1 select_reduce_fusion.3
  1.7 0.2 select_reduce_fusion
  1.9 0.1 select_reduce_fusion.1
  2.0 0.2 compare_reduce_fusion
  2.2 0.1 select_reduce_fusion.2
  2.3 0.6 concatenate.3.tab
  2.9 102.0 %refresh.1 = (f32[16,64,512]{2,1,0:T(8,128)S(1)}, f32[1,1,3,512,512]{4,3,2,1,0:T(8,128)S(1)}, f32[1,1,3,512,512]{4,3,2,1,0:T(8,128)S(1)}, bf16[1,1,3,512,512]{4,...) custom-call(s32[91]{0:T(128)} %concatenate.3.tab, f32[16,64,512]{2,1,0:T(8,128)} %grad.1, ...), custom_call_target="tpu_custom_call" | custom-call | flops 20132659200 | bytes 23068672 | tf_op jit(solution)/shard_map/refresh/pallas_call | solution.py:302
  105.0 0.0 copy-start
  105.0 1.7 copy-done
  106.6 0.0 copy-start.1
  106.6 1.7 copy-done.1
  108.3 0.0 copy-start.2
  108.3 1.3 copy-done.2
  109.7 0.0 copy-start.3
  109.7 1.2 copy-done.3
  110.9 0.0 copy-start.4
  110.9 1.1 copy-done.4
  112.1 350.5 %finish.1 = (f32[16,64,512]{2,1,0:T(8,128)}, f32[1,1,3,512,512]{4,3,2,1,0:T(8,128)}, f32[1,1,3,512,512]{4,3,2,1,0:T(8,128)}, bf16[1,1,3,512,512]{4,3,2,1,0:T(8,128)(2,1)}, bf16[1,1,3,512,512]{4,3,2,1,0:T(8,128)(2,1)}) custom-call(f32[16,64,512]{2,1,0:T(8,128)} %copy-done.2, f32[1,1,3,512,512]{4,3,2,1,0:T(8,128)} %copy-done, ...), custom_call_target="tpu_custom_call" | custom-call | tf_op jit(solution)/shard_map/finish/pallas_call | solution.py:314
  (6 shorter events, 0.1 us)
Async XLA Ops:
  105.0 1.7 copy-start
  106.6 1.7 copy-start.1
  108.3 1.3 copy-start.2
  109.7 1.2 copy-start.3
  110.9 1.1 copy-start.4

commit v3 on v2

--- a/solution.py
+++ b/solution.py
@@ -16,8 +16,14 @@
 SIDE = 4
 GATHER = ((0, 8), (8, 8), (16, 8), (24, 8), (32, 16), (48, 16))
 RETURN = ((0, 16), (16, 16), (32, 16), (48, 8), (56, 8))
-LATE = 4
-EARLY = 2
+INWARD = (
+    (0, 0, 2, 0, 0), (1, 0, 2, 1, 1), (2, 0, 2, 2, 2), (3, 0, 2, 3, 3),
+    (4, 0, 1, 4, 4), (5, 0, 0, 5, 5), (5, 1, 1, 5, 5), (5, 2, 2, 4, 5),
+)
+OUTWARD = (
+    (0, 0, 0, 0), (0, 0, 0, 1), (1, 1, 1, 0), (2, 2, 2, 0), (2, 1, 2, 1), (2, 0, 2, 2), (2, 0, 2, 3), (2, 0, 2, 4),
+)
+AHEAD = 3
 TINY = 2.0**-48
 
 SEND1, SLOT2, SLOT3, RANK3, ORDER4, LIVE = 0, 16, 40, 56, 72, 88
@@ -123,19 +129,23 @@
     lax.fori_loop(1, RANKS, greet_dp, 0)
     pl.semaphore_wait(barrier, GROUPS - 1 + RANKS - 1)
 
-    for i, (a, n) in enumerate(GATHER):
+    def first(i):
         grad_in[i].wait()
-        rows = pl.ds(a, n)
+        rows = pl.ds(*GATHER[i])
         recv1[i][0] = staged[i][tab[SEND1]]
 
-        def step1(k, carry, i=i, rows=rows):
+        def step1(k, carry):
             send1[k, rows, :] = staged[i][tab[SEND1 + k]]
             remote(send1.at[k, rows], recv1[i].at[k], s1, r1.at[i], mp_peer(k)).start()
             return carry
 
         lax.fori_loop(1, GROUPS, step1, 0)
 
-    def second(i, slots):
+    def region(first_chunk, last_chunk):
+        start = GATHER[first_chunk][0]
+        return pl.ds(start, sum(GATHER[last_chunk]) - start)
+
+    def second(i):
         rows = pl.ds(*GATHER[i])
 
         def fill(d, carry):
@@ -144,24 +154,21 @@
                 send2[d, s, rows, :] = recv1[i][tab[SLOT2 + peer * OWN + s]]
             return carry
 
-        def step2(d, carry):
-            fill(d, carry)
-            leave(d, slots, rows, 0 if slots == OWN else 1)
-            return carry
-
-        lax.fori_loop(1, RANKS, step2, 0)
-
-    def leave(d, slots, rows, sem):
-        some = pl.ds(0, slots)
-        remote(send2.at[d, some, rows], gbuf.at[some, rank, rows], s2, r2.at[sem], dp_peer(d)).start()
-
-    late_from = GATHER[LATE][0]
-    late_rows = pl.ds(late_from, ROWS - late_from)
-
-    def step2_late(d, carry):
-        some = pl.ds(OWN - 1, 1)
-        remote(send2.at[d, some, late_rows], gbuf.at[some, rank, late_rows], s2, r2.at[2], dp_peer(d)).start()
-        return carry
+        for order, (after, first_slot, last_slot, first_chunk, last_chunk) in enumerate(INWARD):
+            if after != i:
+                continue
+            slots, part = pl.ds(first_slot, last_slot - first_slot + 1), region(first_chunk, last_chunk)
+
+            def step2(d, carry, order=order, slots=slots, part=part, filled=fill):
+                if filled is not None:
+                    filled(d, carry)
+                remote(
+                    send2.at[d, slots, part], gbuf.at[slots, rank, part], s2, r2.at[order], dp_peer(d)
+                ).start()
+                return carry
+
+            lax.fori_loop(1, RANKS, step2, 0)
+            fill = None
 
     def own_rows(i):
         a, n = GATHER[i]
@@ -178,11 +185,13 @@
         x5[side, s, 0] = high
         x5[side, s, 1] = low
 
+    for i in range(AHEAD):
+        first(i)
     for i in range(ng):
         wait_recv(recv1[i].at[pl.ds(1, GROUPS - 1)], r1.at[i])
-        second(i, OWN if i < LATE else OWN - 1)
-        if i == ng - 1:
-            lax.fori_loop(1, RANKS, step2_late, 0)
+        second(i)
+        if i + AHEAD < ng:
+            first(i + AHEAD)
         own_rows(i)
         if i == 0:
             state_in[0].wait()
@@ -223,17 +232,17 @@
         for s in range(first, first + count):
             recv3[i][s, rank] = send3[s, rank, rows, :]
 
-    early = pl.ds(0, late_from)
-    wait_recv(gbuf.at[:, pl.ds(0, RANKS - 1), early], r2.at[0])
-    wait_recv(gbuf.at[pl.ds(0, OWN - 1), pl.ds(0, RANKS - 1), late_rows], r2.at[1])
-    refresh(0)
-    for i in range(EARLY):
-        back(i, 0, 1)
-    lax.fori_loop(1, OWN - 1, lambda s, carry: (refresh(s), carry)[1], 0)
-    wait_recv(gbuf.at[pl.ds(OWN - 1, 1), pl.ds(0, RANKS - 1), late_rows], r2.at[2])
-    refresh(OWN - 1)
-    for i in range(nr):
-        back(i, *((1, OWN - 1) if i < EARLY else (0, OWN)))
+    waited = set()
+    for s in range(OWN):
+        for order, (_, first_slot, last_slot, first_chunk, last_chunk) in enumerate(INWARD):
+            if first_slot <= s <= last_slot and order not in waited:
+                waited.add(order)
+                slots = pl.ds(first_slot, last_slot - first_slot + 1)
+                wait_recv(gbuf.at[slots, pl.ds(0, RANKS - 1), region(first_chunk, last_chunk)], r2.at[order])
+        refresh(s)
+        for after, first_slot, last_slot, chunk in OUTWARD:
+            if after == s:
+                back(chunk, first_slot, last_slot - first_slot + 1)
 
     for i, (a, n) in enumerate(RETURN):
         rows = pl.ds(a, n)
@@ -296,7 +305,7 @@
             vmem((GROUPS, ROWS, N), f32),
             vmem((2, OWN, 2, N, N), bf16),
         ]
-        + [dma((ng + 4,)), dma, dma((ng,)), dma, dma((3,)), dma, dma((nr,)), dma, dma((nr,))]
+        + [dma((ng + 4,)), dma, dma((ng,)), dma, dma((len(INWARD),)), dma, dma((nr,)), dma, dma((nr,))]
     )
     args = (gradient, stat_left, stat_right, root_left, root_right)
     results = pl.pallas_call(
@@ -314,11 +323,12 @@
     return pl.pallas_call(
         finish,
         out_shape=tuple(jax.ShapeDtypeStruct(x.shape, x.dtype) for x in args),
-        in_specs=[anywhere] * 5,
+        in_specs=[pl.BlockSpec(memory_space=pltpu.VMEM)] * 5,
         out_specs=(anywhere,) * 5,
         scratch_shapes=[dma((5,))],
+        compiler_params=pltpu.CompilerParams(vmem_limit_bytes=4 * 2**20),
         name="finish",
-    )(*results)
+    )(*[pltpu.with_memory_space_constraint(x, pltpu.VMEM) for x in results])
 
 
 def solution(mesh):

time: 463 us -> 105 us (0.23)
  Pallas kernels: 453 us -> 101 us
  local copies, waits for them, and re-layouts: 8.44 us -> 1.35 us
    pallas_call x1, Pallas kernels: 351 us -> 4.33 us  [body(): pl.pallas_call(finish, out_shape=tuple((jax.ShapeDtypeStruct(x.shape, x.d...]
    unnamed x10 -> x0, local copies, waits for them, and re-layouts: 7.08 us -> none
    pallas_call x1, Pallas kernels: 102 us -> 97.1 us  [body(): pl.pallas_call(kernel, out_shape=tuple((pltpu.VMEM(x.shape, x.dtype) for...]
where the time goes in v3:
time: 105 us
  Pallas kernels  101 us (96%)
  local copies, waits for them, and re-layouts  1.35 us (1%)
    pallas_call x1, Pallas kernels, body(): pl.pallas_call(kernel, out_shape=tuple((pltpu.VMEM(x.shape, x.dtype) for...  97.1 us
    pallas_call x1, Pallas kernels, body(): pl.pallas_call(finish, out_shape=tuple((jax.ShapeDtypeStruct(x.shape, x.d...  4.33 us

profile of v3, /device:TPU:1, one launch (start us, length us, event | category | flops | bytes accessed | tf_op | source)
XLA Modules:
  0.0 104.6 jit_solution(6393066263733946657)
XLA Ops:
  0.7 0.8 reshape.100
  1.4 0.1 fusion.1
  1.6 0.1 select_reduce_fusion.3
  1.7 0.2 select_reduce_fusion
  1.9 0.1 select_reduce_fusion.1
  2.0 0.2 compare_reduce_fusion
  2.2 0.1 select_reduce_fusion.2
  2.3 0.6 concatenate.3.tab
  2.9 97.1 %refresh.1 = (f32[16,64,512]{2,1,0:T(8,128)S(1)}, f32[1,1,3,512,512]{4,3,2,1,0:T(8,128)S(1)}, f32[1,1,3,512,512]{4,3,2,1,0:T(8,128)S(1)}, bf16[1,1,3,512,512]{4,...) custom-call(s32[91]{0:T(128)} %concatenate.3.tab, f32[16,64,512]{2,1,0:T(8,128)} %grad.1, ...), custom_call_target="tpu_custom_call" | custom-call | flops 20132659200 | bytes 23068672 | tf_op jit(solution)/shard_map/refresh/pallas_call | solution.py:311
  100.1 4.3 %finish.1 = (f32[16,64,512]{2,1,0:T(8,128)}, f32[1,1,3,512,512]{4,3,2,1,0:T(8,128)}, f32[1,1,3,512,512]{4,3,2,1,0:T(8,128)}, bf16[1,1,3,512,512]{4,3,2,1,0:T(8,128)(2,1)}, bf16[1,1,3,512,512]{4,3,2,1,0:T(8,128)(2,1)}) custom-call(f32[16,64,512]{2,1,0:T(8,128)S(1)} %get-tuple-element.10.refs_0_, f32[1,1,3,512,512]{4,3,2,1,0:T(8,128)S(1)} %get-tuple-element.11.refs_1_, ...), custom_call_target="tpu_custom_call" | custom-call | tf_op jit(solution)/shard_map/finish/pallas_call | solution.py:323
  (6 shorter events, 0.1 us)

commit v4 on v3

--- a/solution.py
+++ b/solution.py
@@ -20,44 +20,30 @@
     (0, 0, 2, 0, 0), (1, 0, 2, 1, 1), (2, 0, 2, 2, 2), (3, 0, 2, 3, 3),
     (4, 0, 1, 4, 4), (5, 0, 0, 5, 5), (5, 1, 1, 5, 5), (5, 2, 2, 4, 5),
 )
+PARTS = (((0, 64),), ((0, 64),), ((0, 16), (16, 48)))
 OUTWARD = (
-    (0, 0, 0, 0), (0, 0, 0, 1), (1, 1, 1, 0), (2, 2, 2, 0), (2, 1, 2, 1), (2, 0, 2, 2), (2, 0, 2, 3), (2, 0, 2, 4),
+    (0, 0, 0, 0, 0), (0, 0, 0, 0, 1), (1, 0, 1, 1, 0), (2, 0, 2, 2, 0),
+    (2, 1, 1, 2, 1), (2, 1, 0, 2, 2), (2, 1, 0, 2, 3), (2, 1, 0, 2, 4),
 )
 AHEAD = 3
 TINY = 2.0**-48
 
-SEND1, SLOT2, SLOT3, RANK3, ORDER4, LIVE = 0, 16, 40, 56, 72, 88
-
-
-def tables(owner, group, rank):
-    table = owner.reshape(GROUPS, GROUPS)
-    of_group, of_rank = table % GROUPS, table // GROUPS
-    each = jnp.arange(GROUPS, dtype=jnp.int32)
-
-    def away(target, source):
-        dz = (target // SIDE - source // SIDE) % SIDE
-        dy = (target % SIDE - source % SIDE) % SIDE
-        return dz * SIDE + dy
-
-    mine = lax.dynamic_index_in_dim(of_group, group, 0, keepdims=False)
-    sent_to = away(mine, group)
-    send1 = jnp.sum(jnp.where(sent_to[None, :] == each[:, None], each[None, :], 0), axis=1)
-    rank_of = jnp.sum(jnp.where(of_group == group, of_rank, 0), axis=1)
-    before = (rank_of[:, None] == rank_of[None, :]) & (each[:, None] > each[None, :])
-    slot_of = jnp.sum(before.astype(jnp.int32), axis=1)
-    place = rank_of * OWN + slot_of
-    came = away(group, each)
-    places = jnp.arange(RANKS * OWN, dtype=jnp.int32)
-    hit = place[None, :] == places[:, None]
-    slot2 = jnp.sum(jnp.where(hit, came[None, :], 0), axis=1)
-    goes = away(each, group)
-    met = goes[None, :] == each[:, None]
-    slot3 = jnp.sum(jnp.where(met, slot_of[None, :], 0), axis=1)
-    rank3 = jnp.sum(jnp.where(met, rank_of[None, :], 0), axis=1)
-    order4 = away(group, mine)
-    slots = jnp.arange(OWN, dtype=jnp.int32)
-    live = jnp.any(place[None, :] == (rank * OWN + slots)[:, None], axis=1).astype(jnp.int32)
-    return jnp.concatenate([send1, slot2, slot3, rank3, order4, live]).astype(jnp.int32)
+SLOTS = OWN * RANKS
+SEND1, RANK_OF, SLOT_OF, SLOT2, LIVE = 0, GROUPS, 2 * GROUPS, 3 * GROUPS, 3 * GROUPS + SLOTS
+
+
+def away(target, source):
+    dz = lax.rem(lax.div(target, SIDE) - lax.div(source, SIDE) + SIDE, SIDE)
+    dy = lax.rem(lax.rem(target, SIDE) - lax.rem(source, SIDE) + SIDE, SIDE)
+    return dz * SIDE + dy
+
+
+def within(index, size):
+    return jnp.minimum(jnp.maximum(index, 0), size - 1)
+
+
+def total(terms):
+    return functools.reduce(lambda x, y: x + y, terms)
 
 
 def split(x):
@@ -74,13 +60,13 @@
     return dot(ah, bh) + (dot(ah, bl) + dot(al, bh))
 
 
-def kernel(tab, grad, stat_l, stat_r, root_l, root_r, outv, new_sl, new_sr, new_rl, new_rr, *scratch):
+def kernel(owner, grad, stat_l, stat_r, root_l, root_r, outv, new_sl, new_sr, new_rl, new_rr, *scratch):
     ng, nr = len(GATHER), len(RETURN)
     scratch = list(scratch)
     take = lambda count: [scratch.pop(0) for _ in range(count)]
     staged, recv1, recv3, recv4 = take(ng), take(ng), take(nr), take(nr)
     send1, send2, gbuf, send3, send4, x5 = take(6)
-    in_sem, s1, r1, s2, r2, s3, r3, s4, r4 = take(9)
+    in_sem, s1, r1, s2, r2, s3, r3, s4, r4, tab = take(10)
 
     st, rt = (new_sl.at[0, 0], new_sr.at[0, 0]), (new_rl.at[0, 0], new_rr.at[0, 0])
     rank, group = lax.axis_index("dp"), lax.axis_index("mp")
@@ -115,6 +101,31 @@
     for copy in grad_in + state_in:
         copy.start()
 
+    def choose_first(k, carry):
+        target = mp_peer(k)[1]
+        tab[SEND1 + k] = total(
+            jnp.where(lax.rem(owner[group * GROUPS + j], GROUPS) == target, j, 0) for j in range(GROUPS)
+        )
+        return carry
+
+    def choose_rank(g, carry):
+        here = [owner[g * GROUPS + j] for j in range(GROUPS)]
+        tab[RANK_OF + g] = total(jnp.where(lax.rem(o, GROUPS) == group, lax.div(o, GROUPS), 0) for o in here)
+        return carry
+
+    def choose_slot(g, carry):
+        mine = tab[RANK_OF + g]
+        tab[SLOT_OF + g] = total(
+            jnp.where((tab[RANK_OF + c] == mine) & (c < g), 1, 0) for c in range(GROUPS)
+        )
+        return carry
+
+    def choose_second(p, carry):
+        places = [tab[RANK_OF + g] * OWN + tab[SLOT_OF + g] for g in range(GROUPS)]
+        tab[SLOT2 + p] = total(jnp.where(places[g] == p, away(group, g), 0) for g in range(GROUPS))
+        tab[LIVE + p] = total(jnp.where(places[g] == p, 1, 0) for g in range(GROUPS))
+        return carry
+
     barrier = pltpu.get_barrier_semaphore()
 
     def greet_mp(k, carry):
@@ -127,15 +138,16 @@
 
     lax.fori_loop(1, GROUPS, greet_mp, 0)
     lax.fori_loop(1, RANKS, greet_dp, 0)
+    lax.fori_loop(0, GROUPS, choose_first, 0)
     pl.semaphore_wait(barrier, GROUPS - 1 + RANKS - 1)
 
     def first(i):
         grad_in[i].wait()
         rows = pl.ds(*GATHER[i])
-        recv1[i][0] = staged[i][tab[SEND1]]
+        recv1[i][0] = staged[i][within(tab[SEND1], GROUPS)]
 
         def step1(k, carry):
-            send1[k, rows, :] = staged[i][tab[SEND1 + k]]
+            send1[k, rows, :] = staged[i][within(tab[SEND1 + k], GROUPS)]
             remote(send1.at[k, rows], recv1[i].at[k], s1, r1.at[i], mp_peer(k)).start()
             return carry
 
@@ -151,7 +163,7 @@
         def fill(d, carry):
             peer = (rank + d) % RANKS
             for s in range(OWN):
-                send2[d, s, rows, :] = recv1[i][tab[SLOT2 + peer * OWN + s]]
+                send2[d, s, rows, :] = recv1[i][within(tab[SLOT2 + peer * OWN + s], GROUPS)]
             return carry
 
         for order, (after, first_slot, last_slot, first_chunk, last_chunk) in enumerate(INWARD):
@@ -173,7 +185,7 @@
     def own_rows(i):
         a, n = GATHER[i]
         for s in range(OWN):
-            gbuf[s, rank, pl.ds(a, n), :] = recv1[i][tab[SLOT2 + rank * OWN + s]]
+            gbuf[s, rank, pl.ds(a, n), :] = recv1[i][within(tab[SLOT2 + rank * OWN + s], GROUPS)]
 
     def power(t):
         side = t % 2
@@ -187,6 +199,9 @@
 
     for i in range(AHEAD):
         first(i)
+    lax.fori_loop(0, GROUPS, choose_rank, 0)
+    lax.fori_loop(0, GROUPS, choose_slot, 0)
+    lax.fori_loop(0, SLOTS, choose_second, 0)
     for i in range(ng):
         wait_recv(recv1[i].at[pl.ds(1, GROUPS - 1)], r1.at[i])
         second(i)
@@ -202,23 +217,40 @@
 
     eye = lax.broadcasted_iota(jnp.int32, (N, N), 0) == lax.broadcasted_iota(jnp.int32, (N, N), 1)
 
-    def newton(side, s, new, taken):
+    def shift(side, s, new, taken):
         scale = jnp.sum(jnp.where(eye, new, 0.0)) / N
-        shifted = split(new / scale + jnp.where(eye, 0.001, 0.0))
-        moved = dot3((x5[side, s, 0], x5[side, s, 1]), shifted)
-        inverse = 1.25 * rt[side][s].astype(jnp.float32) - (0.25 / TINY) * moved
         st[side][s] = jnp.where(taken, new, 0.0)
-        rt[side][s] = jnp.where(taken, inverse, 0.0).astype(jnp.bfloat16)
-        return inverse
+        return split(new / scale + jnp.where(eye, 0.001, 0.0))
+
+    def rows_of(x, part):
+        return x.reshape(RANKS, ROWS, N)[:, part[0] : sum(part)].reshape(RANKS * part[1], N)
+
+    def newton(side, s, shifted, taken, part):
+        high, low = (rows_of(x5[side, s, i], part) for i in range(2))
+        moved = dot3((high, low), shifted)
+        inverse = 1.25 * rows_of(rt[side][s], part).astype(jnp.float32) - (0.25 / TINY) * moved
+        kept = jnp.where(taken, inverse, 0.0).astype(jnp.bfloat16)
+        if part == (0, ROWS):
+            rt[side][s] = kept
+        else:
+            for e in range(RANKS):
+                rt[side][s, pl.ds(e * ROWS + part[0], part[1]), :] = kept[e * part[1] : (e + 1) * part[1]]
+        return split(inverse)
 
     def refresh(s):
-        taken = tab[LIVE + s] > 0
+        taken = tab[LIVE + rank * OWN + s] > 0
         g32 = gbuf[s].reshape(N, N)
         g, gt = split(g32), split(g32.T)
-        inv_l = newton(0, s, 0.95 * st[0][s] + dot3(g, gt), taken)
-        inv_r = newton(1, s, 0.95 * st[1][s] + dot3(gt, g), taken)
-        result = dot3(split(dot3(split(inv_l), g)), split(inv_r))
-        send3[s] = result.reshape(RANKS, ROWS, N)
+        shifted_r = shift(1, s, 0.95 * st[1][s] + dot3(gt, g), taken)
+        inv_r = newton(1, s, shifted_r, taken, (0, ROWS))
+        shifted_l = shift(0, s, 0.95 * st[0][s] + dot3(g, gt), taken)
+        for p, part in enumerate(PARTS[s]):
+            inv_l = newton(0, s, shifted_l, taken, part)
+            result = dot3(split(dot3(inv_l, g)), inv_r)
+            send3[s, :, pl.ds(*part), :] = result.reshape(RANKS, part[1], N)
+            for after, after_part, first_slot, last_slot, chunk in OUTWARD:
+                if (after, after_part) == (s, p):
+                    back(chunk, first_slot, last_slot - first_slot + 1)
 
     def back(i, first, count):
         rows, some = pl.ds(*RETURN[i]), pl.ds(first, count)
@@ -240,16 +272,14 @@
                 slots = pl.ds(first_slot, last_slot - first_slot + 1)
                 wait_recv(gbuf.at[slots, pl.ds(0, RANKS - 1), region(first_chunk, last_chunk)], r2.at[order])
         refresh(s)
-        for after, first_slot, last_slot, chunk in OUTWARD:
-            if after == s:
-                back(chunk, first_slot, last_slot - first_slot + 1)
 
     for i, (a, n) in enumerate(RETURN):
         rows = pl.ds(a, n)
         wait_recv(recv3[i].at[:, pl.ds(0, RANKS - 1)], r3.at[i])
 
         def pick(k, i=i):
-            return recv3[i][tab[SLOT3 + k], tab[RANK3 + k]]
+            g = mp_peer(k)[1]
+            return recv3[i][within(tab[SLOT_OF + g], OWN), within(tab[RANK_OF + g], RANKS)]
 
         recv4[i][0] = pick(0)
 
@@ -265,7 +295,8 @@
         wait_recv(recv4[i].at[pl.ds(1, GROUPS - 1)], r4.at[i])
 
         def step5(j, carry, i=i, rows=rows):
-            outv[j, rows, :] = recv4[i][tab[ORDER4 + j]]
+            source = away(group, lax.rem(owner[group * GROUPS + j], GROUPS))
+            outv[j, rows, :] = recv4[i][within(source, GROUPS)]
             return carry
 
         lax.fori_loop(0, GROUPS, step5, 0)
@@ -286,8 +317,6 @@
 
 
 def body(gradient, owner, stat_left, stat_right, root_left, root_right):
-    group, rank = lax.axis_index("mp"), lax.axis_index("dp")
-    tab = tables(owner, group, rank)
     f32, bf16 = jnp.float32, jnp.bfloat16
     ng, nr = len(GATHER), len(RETURN)
     vmem, dma = pltpu.VMEM, pltpu.SemaphoreType.DMA
@@ -305,7 +334,7 @@
             vmem((GROUPS, ROWS, N), f32),
             vmem((2, OWN, 2, N, N), bf16),
         ]
-        + [dma((ng + 4,)), dma, dma((ng,)), dma, dma((len(INWARD),)), dma, dma((nr,)), dma, dma((nr,))]
+        + [dma((ng + 4,)), dma, dma((ng,)), dma, dma((len(INWARD),)), dma, dma((nr,)), dma, dma((nr,)), pltpu.SMEM((LIVE + SLOTS,), jnp.int32)]
     )
     args = (gradient, stat_left, stat_right, root_left, root_right)
     results = pl.pallas_call(
@@ -319,7 +348,7 @@
         ),
         cost_estimate=pl.CostEstimate(flops=75 * 2 * N**3, bytes_accessed=22 * 2**20, transcendentals=0),
         name="refresh",
-    )(tab, *args)
+    )(owner, *args)
     return pl.pallas_call(
         finish,
         out_shape=tuple(jax.ShapeDtypeStruct(x.shape, x.dtype) for x in args),

time: 105 us -> 101 us (0.962)
  local copies, waits for them, and re-layouts: 1.35 us -> 0 us
    pallas_call x1, Pallas kernels: 97.1 us -> 95.7 us  [body(): pl.pallas_call(kernel, out_shape=tuple((pltpu.VMEM(x.shape, x.dtype) for...]
where the time goes in v4:
time: 101 us
  Pallas kernels  100 us (99%)
    pallas_call x1, Pallas kernels, body(): pl.pallas_call(kernel, out_shape=tuple((pltpu.VMEM(x.shape, x.dtype) for...  95.7 us
    pallas_call x1, Pallas kernels, body(): pl.pallas_call(finish, out_shape=tuple((jax.ShapeDtypeStruct(x.shape, x.d...  4.33 us

profile of v4, /device:TPU:1, one launch (start us, length us, event | category | flops | bytes accessed | tf_op | source)
XLA Modules:
  0.0 100.8 jit_solution(6897960116109609528)
XLA Ops:
  0.6 95.7 %refresh.1 = (f32[16,64,512]{2,1,0:T(8,128)S(1)}, f32[1,1,3,512,512]{4,3,2,1,0:T(8,128)S(1)}, f32[1,1,3,512,512]{4,3,2,1,0:T(8,128)S(1)}, bf16[1,1,3,512,512]{4,...) custom-call(s32[256]{0:T(256)} %owner.1, f32[16,64,512]{2,1,0:T(8,128)} %grad.1, f32[1,1,3,512,512]{4,3,2,1,0:T(8,128)} %stat_l.1, ...), custom_call_target="tpu_custom_call" | custom-call | flops 20132659200 | bytes 23068672 | tf_op jit(solution)/shard_map/refresh/pallas_call | solution.py:340
  96.3 4.3 %finish.1 = (f32[16,64,512]{2,1,0:T(8,128)}, f32[1,1,3,512,512]{4,3,2,1,0:T(8,128)}, f32[1,1,3,512,512]{4,3,2,1,0:T(8,128)}, bf16[1,1,3,512,512]{4,3,2,1,0:T(8,128)(2,1)}, bf16[1,1,3,512,512]{4,3,2,1,0:T(8,128)(2,1)}) custom-call(f32[16,64,512]{2,1,0:T(8,128)S(1)} %get-tuple-element.10.refs_0_, f32[1,1,3,512,512]{4,3,2,1,0:T(8,128)S(1)} %get-tuple-element.11.refs_1_, ...), custom_call_target="tpu_custom_call" | custom-call | tf_op jit(solution)/shard_map/finish/pallas_call | solution.py:352

commit v5 on v4

--- a/solution.py
+++ b/solution.py
@@ -14,18 +14,20 @@
 RANKS = 8
 GROUPS = 16
 SIDE = 4
-GATHER = ((0, 8), (8, 8), (16, 8), (24, 8), (32, 16), (48, 16))
-RETURN = ((0, 16), (16, 16), (32, 16), (48, 8), (56, 8))
+GATHER = (
+    (0, 8, 0, 256), (0, 8, 256, 256), (8, 8, 0, N), (16, 8, 0, N), (24, 8, 0, N), (32, 16, 0, N), (48, 16, 0, N),
+)
+RETURN = ((0, 16, 0, N), (16, 16, 0, N), (32, 16, 0, N), (48, 8, 0, N), (56, 8, 0, 256), (56, 8, 256, 256))
 INWARD = (
-    (0, 0, 2, 0, 0), (1, 0, 2, 1, 1), (2, 0, 2, 2, 2), (3, 0, 2, 3, 3),
-    (4, 0, 1, 4, 4), (5, 0, 0, 5, 5), (5, 1, 1, 5, 5), (5, 2, 2, 4, 5),
+    (0, 0, 2, 0, 0), (1, 0, 2, 1, 1), (2, 0, 2, 2, 2), (3, 0, 2, 3, 3), (4, 0, 2, 4, 4),
+    (5, 0, 1, 5, 5), (6, 0, 0, 6, 6), (6, 1, 1, 6, 6), (6, 2, 2, 5, 6),
 )
 PARTS = (((0, 64),), ((0, 64),), ((0, 16), (16, 48)))
 OUTWARD = (
-    (0, 0, 0, 0, 0), (0, 0, 0, 0, 1), (1, 0, 1, 1, 0), (2, 0, 2, 2, 0),
-    (2, 1, 1, 2, 1), (2, 1, 0, 2, 2), (2, 1, 0, 2, 3), (2, 1, 0, 2, 4),
+    (0, 0, 0, 0, 0), (0, 0, 0, 0, 1), (1, 0, 1, 1, 0), (1, 0, 1, 1, 1), (2, 0, 2, 2, 0),
+    (2, 1, 2, 2, 1), (2, 1, 0, 2, 2), (2, 1, 0, 2, 3), (2, 1, 0, 2, 4), (2, 1, 0, 2, 5),
 )
-AHEAD = 3
+AHEAD = 4
 TINY = 2.0**-48
 
 SLOTS = OWN * RANKS
@@ -44,6 +46,10 @@
 
 def total(terms):
     return functools.reduce(lambda x, y: x + y, terms)
+
+
+def cut(chunk):
+    return pl.ds(chunk[0], chunk[1]), pl.ds(chunk[2], chunk[3])
 
 
 def split(x):
@@ -90,7 +96,7 @@
         remote(region, region, sem, r1.at[0], dp_peer(1)).wait_send()
 
     grad_in = [
-        pltpu.make_async_copy(grad.at[:, pl.ds(a, n), :], staged[i], in_sem.at[i]) for i, (a, n) in enumerate(GATHER)
+        pltpu.make_async_copy(grad.at[:, *cut(chunk)], staged[i], in_sem.at[i]) for i, chunk in enumerate(GATHER)
     ]
     state_in = [
         pltpu.make_async_copy(src.at[0, 0], dst, in_sem.at[ng + i])
@@ -143,27 +149,29 @@
 
     def first(i):
         grad_in[i].wait()
-        rows = pl.ds(*GATHER[i])
+        rows, columns = cut(GATHER[i])
         recv1[i][0] = staged[i][within(tab[SEND1], GROUPS)]
 
         def step1(k, carry):
-            send1[k, rows, :] = staged[i][within(tab[SEND1 + k], GROUPS)]
-            remote(send1.at[k, rows], recv1[i].at[k], s1, r1.at[i], mp_peer(k)).start()
+            send1[k, rows, columns] = staged[i][within(tab[SEND1 + k], GROUPS)]
+            remote(send1.at[k, rows, columns], recv1[i].at[k], s1, r1.at[i], mp_peer(k)).start()
             return carry
 
         lax.fori_loop(1, GROUPS, step1, 0)
 
     def region(first_chunk, last_chunk):
         start = GATHER[first_chunk][0]
-        return pl.ds(start, sum(GATHER[last_chunk]) - start)
+        end = GATHER[last_chunk][0] + GATHER[last_chunk][1]
+        columns = GATHER[first_chunk][2:] if first_chunk == last_chunk else (0, N)
+        return cut((start, end - start, *columns))
 
     def second(i):
-        rows = pl.ds(*GATHER[i])
+        rows, columns = cut(GATHER[i])
 
         def fill(d, carry):
             peer = (rank + d) % RANKS
             for s in range(OWN):
-                send2[d, s, rows, :] = recv1[i][within(tab[SLOT2 + peer * OWN + s], GROUPS)]
+                send2[d, s, rows, columns] = recv1[i][within(tab[SLOT2 + peer * OWN + s], GROUPS)]
             return carry
 
         for order, (after, first_slot, last_slot, first_chunk, last_chunk) in enumerate(INWARD):
@@ -175,7 +183,7 @@
                 if filled is not None:
                     filled(d, carry)
                 remote(
-                    send2.at[d, slots, part], gbuf.at[slots, rank, part], s2, r2.at[order], dp_peer(d)
+                    send2.at[d, slots, *part], gbuf.at[slots, rank, *part], s2, r2.at[order], dp_peer(d)
                 ).start()
                 return carry
 
@@ -183,9 +191,9 @@
             fill = None
 
     def own_rows(i):
-        a, n = GATHER[i]
+        rows, columns = cut(GATHER[i])
         for s in range(OWN):
-            gbuf[s, rank, pl.ds(a, n), :] = recv1[i][within(tab[SLOT2 + rank * OWN + s], GROUPS)]
+            gbuf[s, rank, rows, columns] = recv1[i][within(tab[SLOT2 + rank * OWN + s], GROUPS)]
 
     def power(t):
         side = t % 2
@@ -211,7 +219,8 @@
         if i == 0:
             state_in[0].wait()
             state_in[1].wait()
-        power(i)
+        if i >= ng - 2 * OWN:
+            power(i - (ng - 2 * OWN))
     state_in[2].wait()
     state_in[3].wait()
 
@@ -253,16 +262,16 @@
                     back(chunk, first_slot, last_slot - first_slot + 1)
 
     def back(i, first, count):
-        rows, some = pl.ds(*RETURN[i]), pl.ds(first, count)
+        (rows, columns), some = cut(RETURN[i]), pl.ds(first, count)
 
         def step3(d, carry):
             peer = (rank + d) % RANKS
-            remote(send3.at[some, peer, rows], recv3[i].at[some, rank], s3, r3.at[i], dp_peer(d)).start()
+            remote(send3.at[some, peer, rows, columns], recv3[i].at[some, rank], s3, r3.at[i], dp_peer(d)).start()
             return carry
 
         lax.fori_loop(1, RANKS, step3, 0)
         for s in range(first, first + count):
-            recv3[i][s, rank] = send3[s, rank, rows, :]
+            recv3[i][s, rank] = send3[s, rank, rows, columns]
 
     waited = set()
     for s in range(OWN):
@@ -270,11 +279,11 @@
             if first_slot <= s <= last_slot and order not in waited:
                 waited.add(order)
                 slots = pl.ds(first_slot, last_slot - first_slot + 1)
-                wait_recv(gbuf.at[slots, pl.ds(0, RANKS - 1), region(first_chunk, last_chunk)], r2.at[order])
+                wait_recv(gbuf.at[slots, pl.ds(0, RANKS - 1), *region(first_chunk, last_chunk)], r2.at[order])
         refresh(s)
 
-    for i, (a, n) in enumerate(RETURN):
-        rows = pl.ds(a, n)
+    for i, chunk in enumerate(RETURN):
+        rows, columns = cut(chunk)
         wait_recv(recv3[i].at[:, pl.ds(0, RANKS - 1)], r3.at[i])
 
         def pick(k, i=i):
@@ -283,20 +292,20 @@
 
         recv4[i][0] = pick(0)
 
-        def step4(k, carry, i=i, rows=rows, pick=pick):
-            send4[k, rows, :] = pick(k)
-            remote(send4.at[k, rows], recv4[i].at[k], s4, r4.at[i], mp_peer(k)).start()
+        def step4(k, carry, i=i, rows=rows, columns=columns, pick=pick):
+            send4[k, rows, columns] = pick(k)
+            remote(send4.at[k, rows, columns], recv4[i].at[k], s4, r4.at[i], mp_peer(k)).start()
             return carry
 
         lax.fori_loop(1, GROUPS, step4, 0)
 
-    for i, (a, n) in enumerate(RETURN):
-        rows = pl.ds(a, n)
+    for i, chunk in enumerate(RETURN):
+        rows, columns = cut(chunk)
         wait_recv(recv4[i].at[pl.ds(1, GROUPS - 1)], r4.at[i])
 
-        def step5(j, carry, i=i, rows=rows):
+        def step5(j, carry, i=i, rows=rows, columns=columns):
             source = away(group, lax.rem(owner[group * GROUPS + j], GROUPS))
-            outv[j, rows, :] = recv4[i][within(source, GROUPS)]
+            outv[j, rows, columns] = recv4[i][within(source, GROUPS)]
             return carry
 
         lax.fori_loop(0, GROUPS, step5, 0)
@@ -322,10 +331,10 @@
     vmem, dma = pltpu.VMEM, pltpu.SemaphoreType.DMA
     anywhere = pl.BlockSpec(memory_space=pl.ANY)
     scratch = (
-        [vmem((GROUPS, n, N), f32) for _, n in GATHER]
-        + [vmem((GROUPS, n, N), f32) for _, n in GATHER]
-        + [vmem((OWN, RANKS, n, N), f32) for _, n in RETURN]
-        + [vmem((GROUPS, n, N), f32) for _, n in RETURN]
+        [vmem((GROUPS, c[1], c[3]), f32) for c in GATHER]
+        + [vmem((GROUPS, c[1], c[3]), f32) for c in GATHER]
+        + [vmem((OWN, RANKS, c[1], c[3]), f32) for c in RETURN]
+        + [vmem((GROUPS, c[1], c[3]), f32) for c in RETURN]
         + [
             vmem((GROUPS, ROWS, N), f32),
             vmem((RANKS, OWN, ROWS, N), f32),

time: 101 us -> 99 us (0.980)
  Pallas kernels: 100 us -> 98.1 us
    pallas_call x1, Pallas kernels: 95.7 us -> 93.7 us  [body(): pl.pallas_call(kernel, out_shape=tuple((pltpu.VMEM(x.shape, x.dtype) for...]
where the time goes in v5:
time: 99 us; the launch traced here: 98.9 us
  Pallas kernels  98.1 us (99%)
    pallas_call x1, Pallas kernels, body(): pl.pallas_call(kernel, out_shape=tuple((pltpu.VMEM(x.shape, x.dtype) for...  93.7 us
    pallas_call x1, Pallas kernels, body(): pl.pallas_call(finish, out_shape=tuple((jax.ShapeDtypeStruct(x.shape, x.d...  4.33 us

profile of v5, /device:TPU:1, one launch (start us, length us, event | category | flops | bytes accessed | tf_op | source)
XLA Modules:
  0.0 98.9 jit_solution(3004686036647915212)
XLA Ops:
  0.6 93.7 %refresh.1 = (f32[16,64,512]{2,1,0:T(8,128)S(1)}, f32[1,1,3,512,512]{4,3,2,1,0:T(8,128)S(1)}, f32[1,1,3,512,512]{4,3,2,1,0:T(8,128)S(1)}, bf16[1,1,3,512,512]{4,...) custom-call(s32[256]{0:T(256)} %owner.1, f32[16,64,512]{2,1,0:T(8,128)} %grad.1, f32[1,1,3,512,512]{4,3,2,1,0:T(8,128)} %stat_l.1, ...), custom_call_target="tpu_custom_call" | custom-call | flops 20132659200 | bytes 23068672 | tf_op jit(solution)/shard_map/refresh/pallas_call | solution.py:349
  94.4 4.3 %finish.1 = (f32[16,64,512]{2,1,0:T(8,128)}, f32[1,1,3,512,512]{4,3,2,1,0:T(8,128)}, f32[1,1,3,512,512]{4,3,2,1,0:T(8,128)}, bf16[1,1,3,512,512]{4,3,2,1,0:T(8,128)(2,1)}, bf16[1,1,3,512,512]{4,3,2,1,0:T(8,128)(2,1)}) custom-call(f32[16,64,512]{2,1,0:T(8,128)S(1)} %get-tuple-element.10.refs_0_, f32[1,1,3,512,512]{4,3,2,1,0:T(8,128)S(1)} %get-tuple-element.11.refs_1_, ...), custom_call_target="tpu_custom_call" | custom-call | tf_op jit(solution)/shard_map/finish/pallas_call | solution.py:361

commit v6 on v5

--- a/solution.py
+++ b/solution.py
@@ -17,15 +17,17 @@
 GATHER = (
     (0, 8, 0, 256), (0, 8, 256, 256), (8, 8, 0, N), (16, 8, 0, N), (24, 8, 0, N), (32, 16, 0, N), (48, 16, 0, N),
 )
-RETURN = ((0, 16, 0, N), (16, 16, 0, N), (32, 16, 0, N), (48, 8, 0, N), (56, 8, 0, 256), (56, 8, 256, 256))
+RETURN = (
+    (0, 8, 0, N), (8, 8, 0, N), (16, 16, 0, N), (32, 16, 0, N), (48, 8, 0, N), (56, 8, 0, 256), (56, 8, 256, 256),
+)
 INWARD = (
     (0, 0, 2, 0, 0), (1, 0, 2, 1, 1), (2, 0, 2, 2, 2), (3, 0, 2, 3, 3), (4, 0, 2, 4, 4),
     (5, 0, 1, 5, 5), (6, 0, 0, 6, 6), (6, 1, 1, 6, 6), (6, 2, 2, 5, 6),
 )
 PARTS = (((0, 64),), ((0, 64),), ((0, 16), (16, 48)))
 OUTWARD = (
-    (0, 0, 0, 0, 0), (0, 0, 0, 0, 1), (1, 0, 1, 1, 0), (1, 0, 1, 1, 1), (2, 0, 2, 2, 0),
-    (2, 1, 2, 2, 1), (2, 1, 0, 2, 2), (2, 1, 0, 2, 3), (2, 1, 0, 2, 4), (2, 1, 0, 2, 5),
+    (0, 0, 0, 0, 0), (0, 0, 0, 0, 1), (0, 0, 0, 0, 2), (1, 0, 1, 1, 0), (1, 0, 1, 1, 1), (1, 0, 1, 1, 2),
+    (2, 0, 2, 2, 0), (2, 0, 2, 2, 1), (2, 1, 2, 2, 2), (2, 1, 0, 2, 3), (2, 1, 0, 2, 4), (2, 1, 0, 2, 5), (2, 1, 0, 2, 6),
 )
 AHEAD = 4
 TINY = 2.0**-48

time: 99 us -> 97.4 us (0.984)
  Pallas kernels: 98.1 us -> 96.5 us
    pallas_call x1, Pallas kernels: 93.7 us -> 92.1 us  [body(): pl.pallas_call(kernel, out_shape=tuple((pltpu.VMEM(x.shape, x.dtype) for...]
where the time goes in v6:
time: 97.4 us; the launch traced here: 97.3 us
  Pallas kernels  96.5 us (99%)
    pallas_call x1, Pallas kernels, body(): pl.pallas_call(kernel, out_shape=tuple((pltpu.VMEM(x.shape, x.dtype) for...  92.1 us
    pallas_call x1, Pallas kernels, body(): pl.pallas_call(finish, out_shape=tuple((jax.ShapeDtypeStruct(x.shape, x.d...  4.33 us

profile of v6, /device:TPU:1, one launch (start us, length us, event | category | flops | bytes accessed | tf_op | source)
XLA Modules:
  0.0 97.3 jit_solution(5677929371992411181)
XLA Ops:
  0.6 92.1 %refresh.1 = (f32[16,64,512]{2,1,0:T(8,128)S(1)}, f32[1,1,3,512,512]{4,3,2,1,0:T(8,128)S(1)}, f32[1,1,3,512,512]{4,3,2,1,0:T(8,128)S(1)}, bf16[1,1,3,512,512]{4,...) custom-call(s32[256]{0:T(256)} %owner.1, f32[16,64,512]{2,1,0:T(8,128)} %grad.1, f32[1,1,3,512,512]{4,3,2,1,0:T(8,128)} %stat_l.1, ...), custom_call_target="tpu_custom_call" | custom-call | flops 20132659200 | bytes 23068672 | tf_op jit(solution)/shard_map/refresh/pallas_call | solution.py:351
  92.8 4.3 %finish.1 = (f32[16,64,512]{2,1,0:T(8,128)}, f32[1,1,3,512,512]{4,3,2,1,0:T(8,128)}, f32[1,1,3,512,512]{4,3,2,1,0:T(8,128)}, bf16[1,1,3,512,512]{4,3,2,1,0:T(8,128)(2,1)}, bf16[1,1,3,512,512]{4,3,2,1,0:T(8,128)(2,1)}) custom-call(f32[16,64,512]{2,1,0:T(8,128)S(1)} %get-tuple-element.10.refs_0_, f32[1,1,3,512,512]{4,3,2,1,0:T(8,128)S(1)} %get-tuple-element.11.refs_1_, ...), custom_call_target="tpu_custom_call" | custom-call | tf_op jit(solution)/shard_map/finish/pallas_call | solution.py:363

commit v7 on v6

--- a/solution.py
+++ b/solution.py
@@ -152,14 +152,14 @@
     def first(i):
         grad_in[i].wait()
         rows, columns = cut(GATHER[i])
-        recv1[i][0] = staged[i][within(tab[SEND1], GROUPS)]
 
         def step1(k, carry):
             send1[k, rows, columns] = staged[i][within(tab[SEND1 + k], GROUPS)]
             remote(send1.at[k, rows, columns], recv1[i].at[k], s1, r1.at[i], mp_peer(k)).start()
             return carry
 
-        lax.fori_loop(1, GROUPS, step1, 0)
+        lax.fori_loop(1, GROUPS, step1, 0, unroll=True)
+        recv1[i][0] = staged[i][within(tab[SEND1], GROUPS)]
 
     def region(first_chunk, last_chunk):
         start = GATHER[first_chunk][0]
@@ -292,14 +292,14 @@
             g = mp_peer(k)[1]
             return recv3[i][within(tab[SLOT_OF + g], OWN), within(tab[RANK_OF + g], RANKS)]
 
-        recv4[i][0] = pick(0)
 
         def step4(k, carry, i=i, rows=rows, columns=columns, pick=pick):
             send4[k, rows, columns] = pick(k)
             remote(send4.at[k, rows, columns], recv4[i].at[k], s4, r4.at[i], mp_peer(k)).start()
             return carry
 
-        lax.fori_loop(1, GROUPS, step4, 0)
+        lax.fori_loop(1, GROUPS, step4, 0, unroll=True)
+        recv4[i][0] = pick(0)
 
     for i, chunk in enumerate(RETURN):
         rows, columns = cut(chunk)

time: 97.4 us -> 97.1 us (level)
  no operation moved by 1% of the time
where the time goes in v7:
time: 97.1 us; the launch traced here: 96.9 us
  Pallas kernels  96.1 us (99%)
    pallas_call x1, Pallas kernels, body(): pl.pallas_call(kernel, out_shape=tuple((pltpu.VMEM(x.shape, x.dtype) for...  91.8 us
    pallas_call x1, Pallas kernels, body(): pl.pallas_call(finish, out_shape=tuple((jax.ShapeDtypeStruct(x.shape, x.d...  4.33 us

profile of v7, /device:TPU:1, one launch (start us, length us, event | category | flops | bytes accessed | tf_op | source)
XLA Modules:
  0.0 96.9 jit_solution(7855445867827163750)
XLA Ops:
  0.6 91.8 %refresh.1 = (f32[16,64,512]{2,1,0:T(8,128)S(1)}, f32[1,1,3,512,512]{4,3,2,1,0:T(8,128)S(1)}, f32[1,1,3,512,512]{4,3,2,1,0:T(8,128)S(1)}, bf16[1,1,3,512,512]{4,...) custom-call(s32[256]{0:T(256)} %owner.1, f32[16,64,512]{2,1,0:T(8,128)} %grad.1, f32[1,1,3,512,512]{4,3,2,1,0:T(8,128)} %stat_l.1, ...), custom_call_target="tpu_custom_call" | custom-call | flops 20132659200 | bytes 23068672 | tf_op jit(solution)/shard_map/refresh/pallas_call | solution.py:351
  92.4 4.3 %finish.1 = (f32[16,64,512]{2,1,0:T(8,128)}, f32[1,1,3,512,512]{4,3,2,1,0:T(8,128)}, f32[1,1,3,512,512]{4,3,2,1,0:T(8,128)}, bf16[1,1,3,512,512]{4,3,2,1,0:T(8,128)(2,1)}, bf16[1,1,3,512,512]{4,3,2,1,0:T(8,128)(2,1)}) custom-call(f32[16,64,512]{2,1,0:T(8,128)S(1)} %get-tuple-element.10.refs_0_, f32[1,1,3,512,512]{4,3,2,1,0:T(8,128)S(1)} %get-tuple-element.11.refs_1_, ...), custom_call_target="tpu_custom_call" | custom-call | tf_op jit(solution)/shard_map/finish/pallas_call | solution.py:363
